TPU v7x, 32 devices: a whole 2x2x4 slice. The times are simulated.
32 devices in a mesh: blk: 16 (over z, x, core), fsdp: 2 (over y).
Axes of the slice: x: 2, y: 2, z: 4, core: 2. Of those that a mesh axis runs over, the one named last changes fastest.
Arguments:
- features: bfloat16 [2, 2, 4096, 256], P(None, 'fsdp', 'blk'), may hold values from -6 to 6
- neighbours: int32 [2, 2, 4096, 32], P(None, 'fsdp', 'blk'), may hold values from 0 to 4095, as said below
- slot_mask: int32 [2, 2, 4096, 32], P(None, 'fsdp', 'blk'), may hold values from 0 to 1, as said below
- projections: bfloat16 [2, 196608], P(None, ('blk', 'fsdp')), may hold values from -0.5 to 0.5
- vectors: bfloat16 [2, 1024], P(None, ('blk', 'fsdp')), may hold values from -2 to 2
- out_cotangent: bfloat16 [2, 2, 4096, 256], P(None, 'fsdp', 'blk'), may hold values from -6 to 6
Outputs:
- layer_output: bfloat16 [2, 2, 4096, 256], P(None, 'fsdp', 'blk')
- input_gradient: float32 [2, 2, 4096, 256], P(None, 'fsdp', 'blk')
- projection_gradient: float32 [2, 196608], P(None, ('blk', 'fsdp'))
- vector_gradient: float32 [2, 1024], P(None, ('blk', 'fsdp'))
Inputs may be any that keep to these rules, and one draw needn't show every extreme that they name: `neighbours`: slot 0 of every node names the node itself. Every slot names a node of the node's own graph. Within a micro-batch and group, the rows below 64 of every device's block of 256 rows form one graph over the whole group; every other graph holds at most 96 nodes that are consecutive among the remaining rows of the group taken in order, so it lies on one device or on two neighbouring ones. `slot_mask`: slot 0 is always 1.
All inputs are finite; a program needn't handle non-finite values.
Results may differ from a plain program's by a relative error of at most 0.018.
Values may be sent and summed in bfloat16 or wider, within the bound.
A program may use at most 256 MiB of HBM per device.

v0:
```python
import jax
import jax.numpy as jnp
from jax import lax
from jax.sharding import PartitionSpec as P

HEADS = 4


epsilon = 1e-05


def smooth_leaky(values):
    return 0.2 * values + 0.8 * jax.nn.silu(values)


def smooth_slope(values):
    sigma = jax.nn.sigmoid(values)
    return 0.2 + 0.8 * (sigma + values * sigma * (1.0 - sigma))


def score_rows(gathered, targets, attn_vector, usable):
    row_count = gathered.shape[0]
    slot_count = gathered.shape[1]
    feature_width = gathered.shape[2]
    summed = gathered.astype(jnp.float32) + targets[:, None, :]
    lifted = smooth_leaky(summed)
    logits = jnp.sum(
        (lifted * attn_vector).reshape(row_count, slot_count, HEADS, feature_width // HEADS),
        axis=-1,
    )
    return (summed, lifted, jnp.where(usable, logits, -1e30))


def one_hot_rows(index_rows, table_rows):
    return (
        index_rows.reshape(-1)[:, None] == jnp.arange(table_rows, dtype=jnp.int32)[None, :]
    ).astype(jnp.bfloat16)


def pick_rows(selector, table):
    return jnp.dot(selector, table, preferred_element_type=jnp.float32).astype(jnp.bfloat16)


def spread_back(selector, values):
    high_part = values.astype(jnp.bfloat16)
    rest = values - high_part.astype(jnp.float32)
    middle_part = rest.astype(jnp.bfloat16)
    low_part = (rest - middle_part.astype(jnp.float32)).astype(jnp.bfloat16)
    dims = (((0,), (0,)), ((), ()))
    total = lax.dot_general(selector, high_part, dims, preferred_element_type=jnp.float32)
    total = total + lax.dot_general(selector, middle_part, dims, preferred_element_type=jnp.float32)
    return total + lax.dot_general(selector, low_part, dims, preferred_element_type=jnp.float32)


def per_device(features, neighbours, slot_mask, projections, vectors, out_cotangent):
    micro_count = features.shape[0]
    row_count = features.shape[2]
    feature_width = features.shape[3]
    layer_count = projections.shape[0]
    slot_count = neighbours.shape[3]
    head_width = feature_width // HEADS
    block_count = lax.axis_size("blk")
    group_nodes = row_count * block_count
    quarter = row_count // 4
    small_rows = row_count - quarter
    big_total = block_count * quarter

    def fetch(layer_index):
        flat_weights, flat_vectors = (
            lax.all_gather(projections[layer_index], ("blk", "fsdp"), axis=0, tiled=True),
            lax.all_gather(vectors[layer_index], ("blk", "fsdp"), axis=0, tiled=True),
        )
        return (
            flat_weights.reshape(3, feature_width, feature_width),
            flat_vectors.astype(jnp.float32).reshape(4, feature_width),
        )

    def split_table(full_rows):
        own_block = lax.axis_index("blk")
        blocks = full_rows.reshape(block_count, row_count, feature_width)
        big_part = blocks[:, :quarter].reshape(big_total, feature_width)
        padded = jnp.pad(blocks[:, quarter:], ((1, 1), (0, 0), (0, 0)))
        rim_part = lax.dynamic_slice_in_dim(padded, own_block, 3, 0).reshape(
            3 * small_rows, feature_width
        )
        return (big_part, rim_part)

    def take_sources(tables, picks):
        big_sel, small_sel = picks
        big_rows = pick_rows(big_sel, tables[0]).reshape(quarter, slot_count, feature_width)
        small_part = pick_rows(small_sel, tables[1]).reshape(small_rows, slot_count, feature_width)
        return jnp.concatenate([big_rows, small_part], axis=0)

    weight_sums = [None] * layer_count
    vector_sums = [None] * layer_count
    outputs = []
    input_grads = []
    for micro_index in range(micro_count):
        weight_list = [fetch(layer_index) for layer_index in range(layer_count)]
        hidden_low = features[micro_index, 0]
        neighbour_rows = neighbours[micro_index, 0]
        selectors_own_block = lax.axis_index("blk")
        selectors_big_rows = neighbour_rows[:quarter]
        selectors_small_part = neighbour_rows[quarter:]
        big_place = selectors_big_rows // row_count * quarter + selectors_big_rows % row_count
        small_place = (selectors_small_part // row_count - selectors_own_block + 1) * small_rows + (
            selectors_small_part % row_count - quarter
        )
        picks = (one_hot_rows(big_place, big_total), one_hot_rows(small_place, 3 * small_rows))
        usable = slot_mask[micro_index, 0][:, :, None] > 0
        saved_list = []
        for layer_index in range(layer_count):
            forward_vector_set = weight_list[layer_index][1]
            projected = jnp.einsum(
                "nd,kde->kne",
                hidden_low,
                weight_list[layer_index][0],
                preferred_element_type=jnp.float32,
            )
            forward_sources_low = projected[0].astype(jnp.bfloat16)
            forward_targets = projected[1]
            residue = projected[2]
            forward_tables = split_table(
                lax.all_gather(forward_sources_low, "blk", axis=0, tiled=True)
            )
            forward_gathered = take_sources(forward_tables, picks)
            forward_summed, forward_lifted, forward_logits = score_rows(
                forward_gathered, forward_targets, forward_vector_set[0], usable
            )
            largest = jnp.max(forward_logits, axis=1, keepdims=True)
            raised = jnp.exp(forward_logits - largest) * usable.astype(jnp.float32)
            totals = jnp.sum(raised, axis=1, keepdims=True)
            forward_shares_low = (raised / totals).astype(jnp.bfloat16)
            forward_log_totals = largest + jnp.log(totals)
            message = jnp.einsum(
                "nsh,nshe->nhe",
                forward_shares_low,
                forward_gathered.reshape(row_count, slot_count, HEADS, head_width),
                preferred_element_type=jnp.float32,
            )
            summed_rows = (
                message.reshape(row_count, feature_width) + forward_vector_set[1] + residue
            )
            centred = summed_rows - jnp.mean(summed_rows, axis=-1, keepdims=True)
            spread = jnp.mean(jnp.square(centred), axis=-1, keepdims=True)
            forward_inverse = lax.rsqrt(spread + epsilon)
            forward_normed = centred * forward_inverse
            forward_shifted = forward_normed * forward_vector_set[2] + forward_vector_set[3]
            activated = jax.nn.elu(forward_shifted)
            activated, saved = (
                activated,
                (
                    hidden_low,
                    forward_targets,
                    forward_sources_low,
                    forward_log_totals,
                    forward_normed,
                    forward_inverse,
                    forward_shifted,
                ),
            )
            saved_list.append(saved)
            hidden_low = activated.astype(jnp.bfloat16)
        outputs.append(hidden_low)
        grad_act = out_cotangent[micro_index, 0].astype(jnp.float32)
        for layer_index in reversed(range(layer_count)):
            vector_set = weight_list[layer_index][1]
            backward_hidden_low, targets, kept_sources, log_totals, normed, inverse, shifted = (
                saved_list[layer_index]
            )
            grad_shift = grad_act * jnp.where(shifted > 0, 1.0, jnp.exp(jnp.minimum(shifted, 0.0)))
            grad_gain = jnp.sum(grad_shift * normed, axis=0)
            grad_offset = jnp.sum(grad_shift, axis=0)
            grad_norm = grad_shift * vector_set[2]
            grad_rows = inverse * (
                grad_norm
                - jnp.mean(grad_norm, axis=-1, keepdims=True)
                - normed * jnp.mean(grad_norm * normed, axis=-1, keepdims=True)
            )
            grad_bias = jnp.sum(grad_rows, axis=0)
            grad_low = grad_rows.astype(jnp.bfloat16)
            backward_tables = split_table(lax.all_gather(kept_sources, "blk", axis=0, tiled=True))
            gathered = take_sources(backward_tables, picks)
            summed, lifted, logits = score_rows(gathered, targets, vector_set[0], usable)
            shares = jnp.exp(logits - log_totals) * usable.astype(jnp.float32)
            shares_low = shares.astype(jnp.bfloat16)
            gathered_heads = gathered.reshape(row_count, slot_count, HEADS, head_width)
            grad_heads = grad_low.reshape(row_count, HEADS, head_width)
            grad_shares = jnp.einsum(
                "nhe,nshe->nsh", grad_heads, gathered_heads, preferred_element_type=jnp.float32
            )
            grad_logits = shares * (
                grad_shares - jnp.sum(shares * grad_shares, axis=1, keepdims=True)
            )
            grad_attn = jnp.einsum(
                "nsh,nshe->he",
                grad_logits,
                lifted.reshape(row_count, slot_count, HEADS, head_width),
            ).reshape(feature_width)
            grad_summed = (
                grad_logits[..., None] * vector_set[0].reshape(HEADS, head_width)
            ).reshape(row_count, slot_count, feature_width) * smooth_slope(summed)
            grad_message = (
                shares_low.astype(jnp.float32)[..., None] * grad_heads.astype(jnp.float32)[:, None]
            )
            backward_grad_gathered = (
                grad_message.reshape(row_count, slot_count, feature_width) + grad_summed
            )
            grad_targets = jnp.sum(grad_summed, axis=1).astype(jnp.bfloat16)
            return_big_sel, return_small_sel = picks
            big_terms = spread_back(
                return_big_sel, backward_grad_gathered[:quarter].reshape(-1, feature_width)
            )
            small_terms = spread_back(
                return_small_sel, backward_grad_gathered[quarter:].reshape(-1, feature_width)
            )
            return_own_block = lax.axis_index("blk")
            empty = jnp.zeros((block_count + 2, small_rows, feature_width), jnp.float32)
            window = lax.dynamic_update_slice_in_dim(
                empty, small_terms.reshape(3, small_rows, feature_width), return_own_block, 0
            )
            full_terms = jnp.concatenate(
                [
                    big_terms.reshape(block_count, quarter, feature_width),
                    window[1 : block_count + 1],
                ],
                axis=1,
            ).reshape(group_nodes, feature_width)
            grad_sources = lax.psum_scatter(
                full_terms.astype(jnp.bfloat16), "blk", scatter_dimension=0, tiled=True
            )
            stacked = jnp.stack([grad_sources, grad_targets, grad_low])
            weight_term = jnp.einsum(
                "nd,kne->kde", backward_hidden_low, stacked, preferred_element_type=jnp.float32
            )
            grad_hidden = jnp.einsum(
                "kne,kde->nd",
                stacked,
                weight_list[layer_index][0],
                preferred_element_type=jnp.float32,
            )
            vector_term = jnp.stack([grad_attn, grad_bias, grad_gain, grad_offset])
            grad_act, weight_term, vector_term = (grad_hidden, weight_term, vector_term)
            reduced_weights = lax.psum_scatter(
                weight_term.reshape(-1), ("blk", "fsdp"), scatter_dimension=0, tiled=True
            )
            reduced_vectors = lax.psum_scatter(
                vector_term.reshape(-1), ("blk", "fsdp"), scatter_dimension=0, tiled=True
            )
            if weight_sums[layer_index] is None:
                weight_sums[layer_index] = reduced_weights
                vector_sums[layer_index] = reduced_vectors
            else:
                weight_sums[layer_index] = weight_sums[layer_index] + reduced_weights
                vector_sums[layer_index] = vector_sums[layer_index] + reduced_vectors
        input_grads.append(grad_act)
    layer_output = jnp.stack(outputs)[:, None]
    input_gradient = jnp.stack(input_grads)[:, None]
    return (layer_output, input_gradient, jnp.stack(weight_sums), jnp.stack(vector_sums))


def solution(mesh):
    return jax.shard_map(
        per_device,
        mesh=mesh,
        in_specs=(
            P(None, "fsdp", "blk", None),
            P(None, "fsdp", "blk", None),
            P(None, "fsdp", "blk", None),
            P(None, ("blk", "fsdp")),
            P(None, ("blk", "fsdp")),
            P(None, "fsdp", "blk", None),
        ),
        out_specs=(
            P(None, "fsdp", "blk", None),
            P(None, "fsdp", "blk", None),
            P(None, ("blk", "fsdp")),
            P(None, ("blk", "fsdp")),
        ),
        check_vma=False,
    )
```

profile of v0, /device:TPU:0, one launch (start us, length us, event | category | flops | bytes accessed | tf_op | source)
XLA Modules:
  0.0 1218.6 jit_solution(2187152244491224185)
XLA Ops:
  8.1 73.9 %all-gather = bf16[1,196608]{1,0:T(2,128)(2,1)S(1)} all-gather(bf16[1,6144]{1,0:T(2,128)(2,1)S(1)} %get-tuple-element.149), channel_id=2, replica_groups=mesh['blk'=16,'fsdp'=2] {'blk','fsdp'}, dimensions={1}, use_global_device_ids=true | all-gather | bytes 405504 | tf_op jit(solution)/shard_map/all_gather | solution.py:70
  82.0 8.2 reduce.12
  96.4 37.5 %all-reduce.12 = (bf16[1024]{0:T(1024)(128)(2,1)S(1)}, bf16[1024]{0:T(1024)(128)(2,1)S(1)}) all-reduce(bf16[1024]{0:T(1024)(128)(2,1)S(1)} %dynamic-update-slice.1, bf16[1024]{0:T(1024)(128)(2,1)S(1)} %dynamic-update-slice), channel_id=7, replica_groups=mesh['blk'=16,'fsdp'=2] {'blk','fsdp'}, use_global_device_ids=true, to_apply=%add.5 | all-reduce | flops 2048 | bytes 8192
  134.0 71.3 %all-gather.3 = bf16[1,196608]{1,0:T(2,128)(2,1)S(1)} all-gather(bf16[1,6144]{1,0:T(2,128)(2,1)S(1)} %get-tuple-element.150), channel_id=5, replica_groups=mesh['blk'=16,'fsdp'=2] {'blk','fsdp'}, dimensions={1}, use_global_device_ids=true | all-gather | bytes 405504 | tf_op jit(solution)/shard_map/all_gather | solution.py:70
  205.3 8.2 reduce.14
  243.5 10.1 copy.489
  268.8 10.4 concatenate.73
  279.2 10.1 copy.476
  298.7 14.9 %multiply_reduce_fusion.15 = (f32[256,32,4]{0,2,1:T(4,128)S(1)}, f32[256,32,4]{0,2,1:T(4,128)S(1)}, bf16[256,32,4,64]{0,3,2,1:T(8,128)(2,1)}, bf16[256,32,4,64]{0,3,2,1:T(8,128)(2,1)}) fusion(f32[4,64]{1,0:T(4,128)} %slice.285, f32[256,4,64]{0,2,1:T(8,128)} %bitcast.592, bf16[192,32,4,64]{0,3,2,1:T(8,128)(2,1)} %copy.489, ...), kind=kLoop, calls=%fused_computation.78 | loop fusion | flops 62849024 | bytes 17564672 | tf_op jit(solution)/shard_map/reduce_sum | solution.py:27
  339.0 7.6 copy.507
  367.9 36.8 %all-gather.15.cloned.1.call-done = bf16[1,4096,256]{1,2,0:T(8,128)(2,1)} async-done(((bf16[1,256,256]{1,2,0:T(8,128)(2,1)}), bf16[1,4096,256]{1,2,0:T(8,128)(2,1)}) %all-gather.15.cloned.1.call-update) | async-done | bytes 2097168 | tf_op jit(solution)/shard_map/all_gather | solution.py:124
  422.0 10.1 copy.495
  447.8 10.2 concatenate.76
  458.0 10.1 copy.482
  481.1 14.9 %multiply_reduce_fusion.14 = (f32[256,32,4]{0,2,1:T(4,128)S(1)}, f32[256,32,4]{0,2,1:T(4,128)S(1)}, bf16[256,32,4,64]{0,3,2,1:T(8,128)(2,1)}, bf16[256,32,4,64]{0,3,2,1:T(8,128)(2,1)}) fusion(f32[4,64]{1,0:T(4,128)} %slice.297, f32[256,4,64]{0,2,1:T(8,128)S(1)} %bitcast.596, bf16[192,32,4,64]{0,3,2,1:T(8,128)(2,1)} %copy.495, ...), kind=kLoop, calls=%fused_computation.73 | loop fusion | flops 62849024 | bytes 17564672 | tf_op jit(solution)/shard_map/reduce_sum | solution.py:27
  535.6 15.4 %fusion.19 = (f32[256,32,256]{0,2,1:T(8,128)S(1)}, f32[256,32,256]{0,2,1:T(8,128)}) fusion(bf16[192,32,256]{0,2,1:T(8,128)(2,1)} %copy.517, bf16[64,32,256]{0,2,1:T(8,128)(2,1)} %copy.516, f32[256,256]{0,1:T(8,128)} %get-tuple-element.125, f32[256,32,4]{0,2,1:T(4,128)} %fusion.179, f32[256,256]{0,1:T(8,128)} %bitcast.600, ...), kind=kLoop, calls=%fused_computation.23 | loop fusion | flops 75497472 | bytes 26739712 | tf_op jit(solution)/shard_map/add | solution.py:207
  559.7 9.3 copy.519
  592.4 8.8 slice.372
  601.2 9.4 copy.500
  635.8 12.2 %dynamic_update_slice.14 = bf16[18,192,256]{1,0,2:T(8,128)(2,1)} dynamic-update-slice(bf16[18,192,256]{1,0,2:T(8,128)(2,1)} %broadcast.939.clone, bf16[3,192,256]{1,0,2:T(4,128)(2,1)S(1)} %copy.520, s32[]{:T(128)S(6)} %select_n.188, s32[]{:T(128)} %constant.123.clone.1, s32[]{:T(128)} %constant.123.clone.1) | dynamic-update-slice | bytes 589828 | tf_op jit(solution)/shard_map/dynamic_update_slice | solution.py:219
  680.9 12.0 dynamic_update_slice.12
  726.2 13.8 %multiply_reduce_fusion.11 = (bf16[256,4,64]{0,2,1:T(8,128)(2,1)}, bf16[256,4,64]{0,2,1:T(8,128)(2,1)}) fusion(f32[256,32,4]{0,2,1:T(4,128)S(1)} %copy-done.76, f32[4,64]{1,0:T(4,128)} %slice.297, f32[256,4,64]{0,2,1:T(8,128)} %bitcast.599, bf16[192,32,4,64]{0,3,2,1:T(8,128)(2,1)} %copy.482, bf16[64,32,4,64]{0,3,2,1:T(8,128)(2,1)} %copy.481, ...), kind=kLoop, calls=%fused_computation.53 | loop fusion | flops 71172096 | bytes 9438208 | tf_op jit(solution)/shard_map/reduce_sum | solution.py:209
  741.4 53.5 %reduce-scatter.5.cloned.1.call-done = bf16[256,256]{0,1:T(8,128)(2,1)} async-done(((bf16[4096,256]{0,1:T(8,128)(2,1)}), bf16[256,256]{0,1:T(8,128)(2,1)}) %reduce-scatter.5.cloned.1.call-update) | async-done | bytes 131088 | tf_op jit(solution)/shard_map/reduce_scatter | solution.py:229
  806.9 14.2 %fusion.21 = (f32[256,32,256]{0,2,1:T(8,128)}, f32[256,32,256]{0,2,1:T(8,128)S(1)}) fusion(bf16[192,32,256]{0,2,1:T(8,128)(2,1)S(1)} %copy-done.21, bf16[64,32,256]{0,2,1:T(8,128)(2,1)} %copy.506, f32[256,256]{0,1:T(8,128)S(1)} %copy-done.81, f32[256]{0:T(256)S(1)} %bitcast.675, f32[256,32,4]{0,2,1:T(4,128)S(1)} %fusion.181, ...), kind=kLoop, calls=%fused_computation.28 | loop fusion | flops 75497472 | bytes 26739712 | tf_op jit(solution)/shard_map/add | solution.py:207
  829.8 9.5 copy.528
  859.4 9.4 copy.509
  914.0 12.4 %dynamic_update_slice.13 = bf16[18,192,256]{1,0,2:T(8,128)(2,1)} dynamic-update-slice(bf16[18,192,256]{1,0,2:T(8,128)(2,1)} %broadcast.939.clone.3, bf16[3,192,256]{1,0,2:T(4,128)(2,1)S(1)} %copy.510, s32[]{:T(128)S(6)} %select_n.188, s32[]{:T(128)} %constant.123.clone.1, s32[]{:T(128)} %constant.123.clone.1) | dynamic-update-slice | bytes 589828 | tf_op jit(solution)/shard_map/dynamic_update_slice | solution.py:219
  955.7 12.2 %dynamic_update_slice.15 = bf16[18,192,256]{1,0,2:T(8,128)(2,1)} dynamic-update-slice(bf16[18,192,256]{1,0,2:T(8,128)(2,1)} %broadcast.939.clone.2, bf16[3,192,256]{1,0,2:T(4,128)(2,1)S(1)} %copy.529, s32[]{:T(128)S(6)} %select_n.188, s32[]{:T(128)} %constant.123.clone.1, s32[]{:T(128)} %constant.123.clone.1) | dynamic-update-slice | bytes 589828 | tf_op jit(solution)/shard_map/dynamic_update_slice | solution.py:219
  1001.9 40.2 %all-reduce.10 = (f32[1024]{0:T(1024)S(1)}, f32[1024]{0:T(1024)S(1)}) all-reduce(f32[1024]{0:T(1024)S(1)} %bitcast.659, f32[1024]{0:T(1024)S(1)} %bitcast.660), channel_id=21, replica_groups=mesh['blk'=16,'fsdp'=2] {'blk','fsdp'}, use_global_device_ids=true, to_apply=%region_55.56.clone | all-reduce | flops 2048 | bytes 16384
  1042.2 13.4 %multiply_reduce_fusion.10 = (bf16[256,4,64]{0,2,1:T(8,128)(2,1)}, bf16[256,4,64]{0,2,1:T(8,128)(2,1)S(1)}) fusion(f32[256,32,4]{0,2,1:T(4,128)S(1)} %copy-done.72, f32[4,64]{1,0:T(4,128)S(1)} %copy-done.122, f32[256,4,64]{0,2,1:T(8,128)S(1)} %bitcast.595, bf16[192,32,4,64]{0,3,2,1:T(8,128)(2,1)} %copy.476, bf16[64,32,4,64]{0,3,2,1:T(8,128)(2,1)} %copy.475, ...), kind=kLoop, calls=%fused_computation.52 | loop fusion | flops 71172096 | bytes 9438208 | tf_op jit(solution)/shard_map/reduce_sum | solution.py:209
  1057.0 15.9 %reduce-scatter.11.cloned.1.call-done = bf16[256,256]{0,1:T(8,128)(2,1)} async-done(((bf16[4096,256]{0,1:T(8,128)(2,1)}), bf16[256,256]{0,1:T(8,128)(2,1)}) %reduce-scatter.11.cloned.1.call-update) | async-done | bytes 131088 | tf_op jit(solution)/shard_map/reduce_scatter | solution.py:229
  1077.9 131.8 %all-reduce.15.cloned.1.call-done = (f32[196608]{0:T(1024)}, f32[196608]{0:T(1024)}) async-done(((f32[196608]{0:T(1024)}, f32[196608]{0:T(1024)}), (f32[196608]{0:T(1024)}, f32[196608]{0:T(1024)})) %all-reduce.15.cloned.1.call-update) | async-done | bytes 1572880
  (590 shorter events, 474.6 us)
Async XLA Ops:
  7.2 88.8 %copy-start.150 = (bf16[2,32]{1,0:T(2,128)(2,1)S(1)}, bf16[2,32]{1,0:T(2,128)(2,1)}, u32[]{:S(2)}) copy-start(bf16[2,32]{1,0:T(2,128)(2,1)} %param.10) | copy-start | bytes 388
  7.2 214.0 %all-gather.17.cloned.1.call-start = ((), (), s32[]{:S(2)}) async-start(), calls=%async_computation.10 | async-start | bytes 2228224 | tf_op jit(solution)/shard_map/all_gather | solution.py:124
  90.3 130.8 %copy-start.44 = (bf16[3,256,256]{2,1,0:T(8,128)(2,1)}, bf16[3,256,256]{2,1,0:T(8,128)(2,1)S(1)}, u32[]{:S(2)}) copy-start(bf16[3,256,256]{2,1,0:T(8,128)(2,1)S(1)} %reshape.1342) | copy-start | bytes 1179652
  91.7 129.5 %copy-start.32 = (f32[3,256,256]{1,2,0:T(8,128)}, f32[3,256,256]{1,2,0:T(8,128)S(1)}, u32[]{:S(2)}) copy-start(f32[3,256,256]{1,2,0:T(8,128)S(1)} %convolution_bitcast_fusion.1) | copy-start | bytes 2359300
  92.4 134.1 %all-gather.13.cloned.1.call-start = ((), (), s32[]{:S(2)}) async-start(), calls=%async_computation.8 | async-start | bytes 2228224 | tf_op jit(solution)/shard_map/all_gather | solution.py:124
  93.7 127.5 %copy-start.30 = (f32[3,256,256]{1,2,0:T(8,128)}, f32[3,256,256]{1,2,0:T(8,128)S(1)}, u32[]{:S(2)}) copy-start(f32[3,256,256]{1,2,0:T(8,128)S(1)} %convolution_bitcast_fusion.3) | copy-start | bytes 2359300
  94.5 268.1 %all-gather.19.cloned.1.call-start = ((), (), s32[]{:S(2)}) async-start(), calls=%async_computation.11 | async-start | bytes 2228224 | tf_op jit(solution)/shard_map/all_gather | solution.py:124
  213.6 113.4 %copy-start.46 = (bf16[3,256,256]{2,1,0:T(8,128)(2,1)}, bf16[3,256,256]{2,1,0:T(8,128)(2,1)S(1)}, u32[]{:S(2)}) copy-start(bf16[3,256,256]{2,1,0:T(8,128)(2,1)S(1)} %reshape.1348) | copy-start | bytes 1179652
  263.1 56.1 %copy-start.14 = (bf16[64,32,4,64]{0,3,2,1:T(8,128)(2,1)}, bf16[64,32,4,64]{0,3,2,1:T(8,128)(2,1)S(1)}, u32[]{:S(2)}) copy-start(bf16[64,32,4,64]{0,3,2,1:T(8,128)(2,1)S(1)} %copy.488) | copy-start | bytes 3145732
  292.0 21.6 %copy-start.40 = (bf16[2048,256]{1,0:T(8,128)(2,1)}, bf16[2048,256]{1,0:T(8,128)(2,1)S(1)}, u32[]{:S(2)}) copy-start(bf16[2048,256]{1,0:T(8,128)(2,1)S(1)} %fusion.92) | copy-start | bytes 3145732
  325.3 79.4 %all-gather.15.cloned.1.call-start = ((), (), s32[]{:S(2)}) async-start(), calls=%async_computation.9 | async-start | bytes 2228224 | tf_op jit(solution)/shard_map/all_gather | solution.py:124
  328.9 411.1 %reduce-scatter.9.cloned.1.call-start = ((), (), s32[]{:S(2)}) async-start(), calls=%async_computation.6 | async-start | bytes 2228224 | tf_op jit(solution)/shard_map/reduce_scatter | solution.py:229
  329.0 20.8 %copy-start.24 = (bf16[6144,256]{1,0:T(8,128)(2,1)S(1)}, bf16[6144,256]{1,0:T(8,128)(2,1)}, u32[]{:S(2)}) copy-start(bf16[6144,256]{1,0:T(8,128)(2,1)} %copy-done.23) | copy-start | bytes 9437188
  337.3 143.8 %copy-start.65 = (f32[1,256,256]{1,2,0:T(8,128)}, f32[1,256,256]{1,2,0:T(8,128)S(1)}, u32[]{:S(2)}) copy-start(f32[1,256,256]{1,2,0:T(8,128)S(1)} %slice.369) | copy-start | bytes 786436
  669.5 125.4 %reduce-scatter.5.cloned.1.call-start = ((), (), s32[]{:S(2)}) async-start(), calls=%async_computation.4 | async-start | bytes 2228224 | tf_op jit(solution)/shard_map/reduce_scatter | solution.py:229
  726.1 68.8 %copy-start.70 = (f32[256,256]{0,1:T(8,128)S(1)}, f32[256,256]{0,1:T(8,128)}, u32[]{:S(2)}) copy-start(f32[256,256]{0,1:T(8,128)} %copy-done.69) | copy-start | bytes 786436
  726.2 68.8 %copy-start.130 = (f32[256]{0:T(256)S(1)}, f32[256]{0:T(256)}, u32[]{:S(2)}) copy-start(f32[256]{0:T(256)} %copy-done.129) | copy-start | bytes 3076
  726.2 68.8 %copy-start.136 = (f32[256]{0:T(256)S(1)}, f32[256]{0:T(256)}, u32[]{:S(2)}) copy-start(f32[256]{0:T(256)} %copy-done.135) | copy-start | bytes 3076
  726.2 329.5 %reduce-scatter.7.cloned.1.call-start = ((), (), s32[]{:S(2)}) async-start(), calls=%async_computation.5 | async-start | bytes 2228224 | tf_op jit(solution)/shard_map/reduce_scatter | solution.py:229
  741.4 61.7 %copy-start.37 = (f32[256,32,4]{0,2,1:T(4,128)S(1)}, f32[256,32,4]{0,2,1:T(4,128)}, u32[]{:S(2)}) copy-start(f32[256,32,4]{0,2,1:T(4,128)} %copy-done.36) | copy-start | bytes 393220
  741.4 61.7 %copy-start.62 = (f32[256,32]{0,1:T(8,128)S(1)}, f32[256,32]{0,1:T(8,128)}, u32[]{:S(2)}) copy-start(f32[256,32]{0,1:T(8,128)} %get-tuple-element.97) | copy-start | bytes 98308
  741.4 61.7 %copy-start.108 = (f32[256,4]{0,1:T(4,128)S(1)}, f32[256,4]{0,1:T(4,128)}, u32[]{:S(2)}) copy-start(f32[256,4]{0,1:T(4,128)} %log_add_fusion.3) | copy-start | bytes 12292
  947.3 125.6 %reduce-scatter.11.cloned.1.call-start = ((), (), s32[]{:S(2)}) async-start(), calls=%async_computation.7 | async-start | bytes 2228224 | tf_op jit(solution)/shard_map/reduce_scatter | solution.py:229
  994.7 47.5 %copy-start.63 = (f32[1,256,256]{1,2,0:T(8,128)S(1)}, f32[1,256,256]{1,2,0:T(8,128)}, u32[]{:S(2)}) copy-start(f32[1,256,256]{1,2,0:T(8,128)} %slice.364) | copy-start | bytes 786436
  994.7 47.5 %copy-start.64 = (f32[1,256,256]{1,2,0:T(8,128)S(1)}, f32[1,256,256]{1,2,0:T(8,128)}, u32[]{:S(2)}) copy-start(f32[1,256,256]{1,2,0:T(8,128)} %slice.346) | copy-start | bytes 786436
  994.7 47.5 %copy-start.72 = (f32[256,32,4]{0,2,1:T(4,128)S(1)}, f32[256,32,4]{0,2,1:T(4,128)}, u32[]{:S(2)}) copy-start(f32[256,32,4]{0,2,1:T(4,128)} %copy-done.71) | copy-start | bytes 393220
  994.7 47.5 %copy-start.122 = (f32[4,64]{1,0:T(4,128)S(1)}, f32[4,64]{1,0:T(4,128)}, u32[]{:S(2)}) copy-start(f32[4,64]{1,0:T(4,128)} %slice.285) | copy-start | bytes 3076
  1001.9 207.8 %all-reduce.15.cloned.1.call-start = ((), (), s32[]{:S(2)}) async-start(), calls=%async_computation.12 | async-start | bytes 3145728
  1042.2 30.7 %copy-start.79 = (bf16[256,256]{0,1:T(8,128)(2,1)S(1)}, bf16[256,256]{0,1:T(8,128)(2,1)}, u32[]{:S(2)}) copy-start(bf16[256,256]{0,1:T(8,128)(2,1)} %copy-done.78) | copy-start | bytes 393220
  1055.6 20.8 %copy-start.45 = (bf16[3,256,256]{2,1,0:T(8,128)(2,1)S(1)}, bf16[3,256,256]{2,1,0:T(8,128)(2,1)}, u32[]{:S(2)}) copy-start(bf16[3,256,256]{2,1,0:T(8,128)(2,1)} %copy-done.44) | copy-start | bytes 1179652
  1055.6 21.1 %copy-start.95 = (bf16[256,4,64]{0,2,1:T(8,128)(2,1)S(1)}, bf16[256,4,64]{0,2,1:T(8,128)(2,1)}, u32[]{:S(2)}) copy-start(bf16[256,4,64]{0,2,1:T(8,128)(2,1)} %get-tuple-element.62) | copy-start | bytes 393220
  1055.6 21.1 %copy-start.151 = (bf16[256,256]{0,1:T(8,128)(2,1)S(1)}, bf16[256,256]{0,1:T(8,128)(2,1)}, u32[]{:S(2)}) copy-start(bf16[256,256]{0,1:T(8,128)(2,1)} %reduce-scatter.7.cloned.1.call-done) | copy-start | bytes 393220
  (131 other events, 975.9 us)
Sparse Core Ops, SparseCore 0:
  92.6 37.2 all-gather.16
  132.0 41.7 all-gather.12
  325.4 37.0 all-gather.18
  364.5 40.1 all-gather.14
  669.7 60.5 reduce-scatter.8
  734.3 60.5 reduce-scatter.4
  947.4 60.5 reduce-scatter.6
  1012.2 60.6 reduce-scatter.10
  1078.4 131.2 all-reduce.14
where the time goes:
time: 1230 us; the launch traced here: 1220 us
  local copies, waits for them, and re-layouts  393 us (32%)
  waiting for transfers between devices  240 us (20%)
  blocking collectives  223 us (18%)
  other arithmetic  213 us (17%)
  matrix products  133 us (11%)
  between operations  16.5 us (1%)
    all_gather x2, blocking collectives, fetch(): lax.all_gather(projections[layer_index], ('blk', 'fsdp'), axis=0, tiled=T...  145 us
    unnamed x10, waiting for transfers between devices  132 us
    concatenate x16, local copies, waits for them, and re-layouts, take_sources(): return jnp.concatenate([big_rows, small_part], axis=0)  99.7 us
    unnamed x2, blocking collectives  77.7 us
    reduce_scatter x4, waiting for transfers between devices, per_device(): lax.psum_scatter(full_terms.astype(jnp.bfloat16), 'blk', scatter_dimensio...  69.4 us
    slice x8, local copies, waits for them, and re-layouts, per_device(): backward_grad_gathered[quarter:].reshape(-1, feature_width)  62.9 us
    dynamic_update_slice x4, local copies, waits for them, and re-layouts, per_device(): lax.dynamic_update_slice_in_dim(empty, small_terms.reshape(3, small_rows,...  48.8 us
    all_gather x4, waiting for transfers between devices, per_device(): lax.all_gather(forward_sources_low, 'blk', axis=0, tiled=True)  38.6 us
  transfers between devices with their start and end apart: 9, of which 5 were waited for; matrix products, arithmetic and copies ran while one was open for 17% of the time, Pallas kernels for 0%

commit v1 on v0

v1 whole, which is shorter than its diff:
```python
import functools
import types

import jax
import jax.numpy as jnp
from jax import lax
from jax.experimental import pallas as pl
from jax.experimental.pallas import tpu as pltpu
from jax.sharding import PartitionSpec as P

HEADS = 4
MICRO = 2
LAYERS = 2
SLOTS = 32
WIDTH = 256
HEAD_WIDTH = WIDTH // HEADS
NODES = 256
BIG = 64
SMALL = NODES - BIG
RIM = 96
EXT = SMALL + 2 * RIM
BLOCKS = NODES // BIG
PAIRS = BIG * SLOTS
STEPS = 8
LANES = PAIRS // STEPS
UNIT = BIG
EPSILON = 1e-05
F32 = jnp.float32
BF16 = jnp.bfloat16
MESH = pl.DeviceIdType.MESH


def nn(left, right):
    return lax.dot_general(
        left, right, (((1,), (0,)), ((), ())), preferred_element_type=F32
    )


def nt(left, right, precision=None):
    return lax.dot_general(
        left, right, (((1,), (1,)), ((), ())), preferred_element_type=F32, precision=precision
    )


def tn(left, right):
    return lax.dot_general(
        left, right, (((0,), (0,)), ((), ())), preferred_element_type=F32
    )


def upper_lanes():
    return lax.broadcasted_iota(jnp.int32, (WIDTH, 128), 1) >= 64


def both_halves(tile):
    return tile + pltpu.roll(tile, 64, 1)


def scratch_plan(depth, shared_weights):
    big_total = 4 * depth * UNIT
    tables = 4 + (LAYERS if shared_weights else 0)
    copies = MICRO if depth <= 4 else 1
    vm = pltpu.VMEM
    plan = dict(
        hot_big=vm((copies, big_total, PAIRS), BF16),
        hot_small=vm((copies, 3, 256, PAIRS), BF16),
        place=vm((MICRO, BLOCKS, STEPS, LANES), jnp.int32),
        used=vm((MICRO, BLOCKS, STEPS, LANES), F32),
        rows_of=vm((4, BLOCKS, WIDTH, PAIRS), BF16),
        shares=vm((4, BLOCKS, STEPS, 8, LANES), F32),
        table=vm((tables, big_total, WIDTH), BF16),
        ext=vm((4, EXT, WIDTH), BF16),
        turned_big=vm((WIDTH, big_total), BF16),
        turned_small=vm((WIDTH, 256), BF16),
        hidden=vm((4, NODES, WIDTH), BF16),
        hidden_t=vm((4, WIDTH, NODES), BF16),
        weights_t=vm((LAYERS, 2 * WIDTH, WIDTH), BF16),
        vecs=vm((LAYERS, 4, WIDTH, 128), F32),
        targets=vm((4, WIDTH, NODES), F32),
        residue=vm((MICRO, WIDTH, NODES), F32),
        doubled=vm((WIDTH, 128), F32),
        scores=vm((STEPS, 8, LANES), F32),
        low_shares=vm((HEADS, STEPS, LANES), F32),
        logit_grads=vm((HEADS, STEPS, LANES), F32),
        message=vm((BLOCKS, WIDTH, 128), F32),
        normed=vm((4, WIDTH, NODES), F32),
        inverse=vm((4, 8, NODES), F32),
        act=vm((WIDTH, NODES), BF16),
        grad_act=vm((MICRO, WIDTH, NODES), F32),
        grad_out=vm((BLOCKS, WIDTH, 128), F32),
        grad_out_t=vm((4, WIDTH, NODES), BF16),
        grad_targets_t=vm((4, WIDTH, NODES), BF16),
        grad_sources_t=vm((4, WIDTH, NODES), BF16),
        grad_targets=vm((BLOCKS, WIDTH, 128), F32),
        terms=vm((WIDTH, PAIRS), BF16),
        grad_ext=vm((EXT, WIDTH), F32),
        grad_small=vm((MICRO, SMALL, WIDTH), F32),
        grad_vecs=vm((LAYERS, 4, WIDTH, 128), F32),
        part=vm((tables, big_total, WIDTH), BF16),
        land_core=vm((tables, big_total // 2, WIDTH), BF16),
        land_x=vm((tables, big_total // 4, WIDTH), BF16),
        land_z=vm((tables, depth - 1, UNIT, WIDTH), BF16),
        land_rim=vm((4, 2, RIM, WIDTH), BF16),
        send_rim=vm((4, 2, RIM, WIDTH), BF16),
        gather_send=pltpu.SemaphoreType.DMA((tables, depth + 4)),
        gather_recv=pltpu.SemaphoreType.DMA((tables, depth + 4)),
        reduce_send=pltpu.SemaphoreType.DMA((tables, depth + 4)),
        reduce_recv=pltpu.SemaphoreType.DMA((tables, depth + 4)),
    )
    if shared_weights:
        plan.update(
            weights=vm((LAYERS, 3 * WIDTH, WIDTH), BF16),
            grad_weights=vm((3 * WIDTH, WIDTH), F32),
            last_unit=vm((LAYERS, UNIT, WIDTH), F32),
            last_send=vm((LAYERS, UNIT, WIDTH), BF16),
            land_y=vm((LAYERS, UNIT // 2, WIDTH), BF16),
        )
    return plan


def step_kernel(depth, shared_weights, names, *refs):
    s = types.SimpleNamespace(**dict(zip(names, refs, strict=True)))
    big_total = 4 * depth * UNIT
    kept = s.hot_big.shape[0]
    me = lax.axis_index("blk")
    core = lax.rem(me, 2)
    along_x = lax.rem(lax.div(me, 2), 2)
    along_z = lax.div(me, 4)
    own_f = lax.axis_index("fsdp")
    block_count = 4 * depth
    before = lax.rem(me + block_count - 1, block_count)
    after = lax.rem(me + 1, block_count)
    z_peers = [
        lax.rem(along_z + k, depth) * 4 + along_x * 2 + core for k in range(1, depth)
    ]
    x_peer = along_z * 4 + (1 - along_x) * 2 + core
    sibling = along_z * 4 + along_x * 2 + (1 - core)

    def unit_row(z, x, c):
        return pl.multiple_of(((c * 2 + x) * depth + z) * UNIT, UNIT)

    own_row = unit_row(along_z, along_x, core)
    z_rows = [
        unit_row(lax.rem(along_z + k, depth), along_x, core) for k in range(1, depth)
    ]

    def remote(src, dst, sems, slot, **where):
        send, recv = sems
        return pltpu.make_async_remote_copy(
            src_ref=src,
            dst_ref=dst,
            send_sem=send.at[slot],
            recv_sem=recv.at[slot],
            device_id=where,
            device_id_type=MESH,
        )

    gather_sems = (s.gather_send, s.gather_recv)
    reduce_sems = (s.reduce_send, s.reduce_recv)
    x_slot, core_slot, low_slot, high_slot, y_slot = (depth - 1 + i for i in range(5))

    def gather_y(q):
        piece = s.table.at[q, pl.ds(pl.multiple_of(own_row + own_f * 32, 32), 32)]
        return remote(piece, piece, gather_sems, (q, y_slot), fsdp=1 - own_f)

    def gather_z(q):
        piece = s.table.at[q, pl.ds(own_row, UNIT)]
        return [
            remote(piece, piece, gather_sems, (q, k), blk=peer)
            for k, peer in enumerate(z_peers)
        ]

    def gather_x(q):
        piece = s.table.at[q, pl.ds(unit_row(0, along_x, core), depth * UNIT)]
        return remote(piece, piece, gather_sems, (q, x_slot), blk=x_peer)

    def gather_core(q):
        piece = s.table.at[q, pl.ds(unit_row(0, 0, core), 2 * depth * UNIT)]
        return remote(piece, piece, gather_sems, (q, core_slot), blk=sibling)

    def gather_rims(p):
        low = remote(
            s.ext.at[p, pl.ds(RIM, RIM)],
            s.ext.at[p, pl.ds(RIM + SMALL, RIM)],
            gather_sems,
            (p, low_slot),
            blk=before,
        )
        high = remote(
            s.ext.at[p, pl.ds(SMALL, RIM)],
            s.ext.at[p, pl.ds(0, RIM)],
            gather_sems,
            (p, high_slot),
            blk=after,
        )
        return [low, high]

    def start(copies):
        for copy in copies if isinstance(copies, list) else [copies]:
            copy.start()

    def finish(copies):
        for copy in copies if isinstance(copies, list) else [copies]:
            copy.wait()

    def reduce_core(q):
        return remote(
            s.part.at[q, pl.ds(unit_row(0, 0, 1 - core), 2 * depth * UNIT)],
            s.land_core.at[q],
            reduce_sems,
            (q, core_slot),
            blk=sibling,
        )

    def reduce_x(q):
        return remote(
            s.part.at[q, pl.ds(unit_row(0, 1 - along_x, core), depth * UNIT)],
            s.land_x.at[q],
            reduce_sems,
            (q, x_slot),
            blk=x_peer,
        )

    def reduce_z(q):
        return [
            remote(
                s.part.at[q, pl.ds(row, UNIT)],
                s.land_z.at[q, k],
                reduce_sems,
                (q, k),
                blk=peer,
            )
            for k, (peer, row) in enumerate(zip(z_peers, z_rows))
        ]

    def reduce_rims(p):
        low = remote(
            s.send_rim.at[p, 0], s.land_rim.at[p, 1], reduce_sems, (p, low_slot), blk=before
        )
        high = remote(
            s.send_rim.at[p, 1], s.land_rim.at[p, 0], reduce_sems, (p, high_slot), blk=after
        )
        return [low, high]

    def reduce_y(layer):
        return remote(
            s.last_send.at[layer, pl.ds(pl.multiple_of((1 - own_f) * 32, 32), 32)],
            s.land_y.at[layer],
            reduce_sems,
            (4 + layer, y_slot),
            fsdp=1 - own_f,
        )

    def add_into(q, row, landed, count):
        def body(i, carry):
            here = pl.ds(pl.multiple_of(row + i * UNIT, UNIT), UNIT)
            there = pl.ds(pl.multiple_of(i * UNIT, UNIT), UNIT)
            s.part[q, here] = (
                s.part[q, here].astype(F32) + landed[q, there].astype(F32)
            ).astype(BF16)
            return carry

        lax.fori_loop(0, count, body, 0)

    def reduce_to_x(q):
        finish(reduce_core(q))
        add_into(q, unit_row(0, 0, core), s.land_core, 2 * depth)
        start(reduce_x(q))

    def reduce_to_z(q):
        finish(reduce_x(q))
        add_into(q, unit_row(0, along_x, core), s.land_x, depth)
        start(reduce_z(q))

    def reduced_unit(q):
        finish(reduce_z(q))
        total = s.part[q, pl.ds(own_row, UNIT)].astype(F32)
        for k in range(depth - 1):
            total = total + s.land_z[q, k].astype(F32)
        return total

    def prepare(m):
        def compact(rows, block):
            part = rows[:, block * BIG : (block + 1) * BIG]
            tile = jnp.concatenate([part[:16], part[16:]], axis=1)
            return jnp.concatenate([tile[:8], tile[8:]], axis=1)

        picked = jnp.transpose(s.neighbours[m])
        usable = jnp.transpose(s.slot_mask[m])
        device = lax.shift_right_logical(picked, 8)
        offset = jnp.bitwise_and(picked, 255)
        z = lax.shift_right_logical(device, 2)
        x = jnp.bitwise_and(lax.shift_right_logical(device, 1), 1)
        c = jnp.bitwise_and(device, 1)
        big_place = ((c * 2 + x) * depth + z) * UNIT + offset
        small_place = (device - me) * SMALL + (offset - BIG)
        for block in range(BLOCKS):
            if block == 0:
                s.place[m, 0] = compact(big_place, 0)
            else:
                s.place[m, block] = compact(small_place + (RIM - (block - 1) * BIG), block)
            s.used[m, block] = compact(usable, block).astype(F32)
        s.hidden[m] = s.features[m]
        s.hidden_t[m] = jnp.transpose(s.features[m])
        s.grad_act[m] = jnp.transpose(s.out_cotangent[m].astype(F32))

    def mark(row, least):
        tile = lax.broadcasted_iota(jnp.int32, (256, LANES), 0)
        return jnp.where(tile == row - least, 1.0, 0.0).astype(BF16)

    def lanes_of(step):
        return pl.ds(pl.multiple_of(step * LANES, LANES), LANES)

    def mark_big(m):
        slot = m if kept > 1 else 0

        def tile(w, carry):
            here = pl.ds(pl.multiple_of(w * 256, 256), 256)
            for step in range(STEPS):
                lanes = pl.ds(step * LANES, LANES)
                row = s.place[m, 0, pl.ds(step, 1), :]
                s.hot_big[slot, here, lanes] = mark(row, w * 256)
            return carry

        lax.fori_loop(0, big_total // 256, tile, 0)

    def mark_small(m):
        def block_body(b, carry):
            for step in range(STEPS):
                lanes = pl.ds(step * LANES, LANES)
                row = s.place[m, b + 1, pl.ds(step, 1), :]
                s.hot_small[m if kept > 1 else 0, b, :, lanes] = mark(row, 0)
            return carry

        lax.fori_loop(0, 3, block_body, 0)

    def load_layer(layer):
        if shared_weights:
            units = {}
            for c in range(2):
                for x in range(2):
                    for z in range(depth):
                        for y in range(2):
                            chunk = ((z * 2 + x) * 2 + c) * 2 + y
                            at = (((c * 2 + x) * depth + z) * 2 + y) * 32
                            units[chunk] = s.table[4 + layer, pl.ds(at, 32)].astype(F32)
            flat = jnp.concatenate(
                [units[i][:24] for i in range(len(units))], axis=0
            ).astype(BF16)
            rows = units[0][24:]
            for i in range(1, len(units)):
                rows = rows + units[i][24:]
            s.weights[layer] = flat
        else:
            rows = s.all_vectors[layer].astype(F32)
        for k in range(2):
            s.weights_t[layer, pl.ds(k * WIDTH, WIDTH)] = jnp.transpose(
                s.weights[layer, pl.ds((k + 1) * WIDTH, WIDTH)]
            )
        which = lax.broadcasted_iota(jnp.int32, (8, 512), 0)
        lane = lax.shift_right_logical(lax.broadcasted_iota(jnp.int32, (8, 512), 1), 7)
        chosen = jnp.where(which == lane, 1.0, 0.0).astype(BF16)
        wide = tn(rows.astype(BF16), chosen)
        for k in range(4):
            s.vecs[layer, k] = wide[:, k * 128 : (k + 1) * 128]

    def project(p, layer, m):
        hidden = s.hidden[p]
        sources = (0.5 * nn(hidden, s.weights[layer, pl.ds(0, WIDTH)])).astype(BF16)
        s.table[p, pl.ds(own_row, UNIT)] = sources[:BIG]
        s.ext[p, pl.ds(RIM, SMALL)] = sources[BIG:]
        start(gather_z(p))
        start(gather_rims(p))
        s.targets[p] = 0.5 * nt(s.weights_t[layer, pl.ds(0, WIDTH)], hidden)
        bias = s.vecs[layer, 1]
        s.residue[m] = nt(s.weights_t[layer, pl.ds(WIDTH, WIDTH)], hidden) + jnp.concatenate(
            [bias, bias], axis=1
        )

    def double(wide, block):
        odd = jnp.bitwise_and(block, 1) == 1
        return jnp.where(upper_lanes() == odd, wide, pltpu.roll(wide, 64, 1))

    def tile_of(block):
        return pl.ds(pl.multiple_of(lax.div(block, 2) * 128, 128), 128)

    def head_rows(h):
        if isinstance(h, int):
            return pl.ds(h * HEAD_WIDTH, HEAD_WIDTH)
        return pl.ds(pl.multiple_of(h * HEAD_WIDTH, HEAD_WIDTH), HEAD_WIDTH)

    def by_head(ref, step, rows):
        for h in range(HEADS):
            ref[h, pl.ds(step, 1), :] = rows[h : h + 1]

    def attend(p, layer, m, block, turned, hot):
        s.doubled[...] = double(s.targets[p, :, tile_of(block)], block)

        def score(step, carry):
            got = nn(turned[...], hot[:, lanes_of(step)])
            s.rows_of[p, block, :, lanes_of(step)] = got.astype(BF16)
            for h in range(HEADS):
                rows = slice(h * HEAD_WIDTH, (h + 1) * HEAD_WIDTH)
                wanted = s.doubled[rows, :]
                attn = s.vecs[layer, 0, rows, :]
                for half in range(2):
                    z = got[rows, half * 128 : (half + 1) * 128] + wanted
                    lifted = z * (jnp.tanh(z) + 1.5)
                    s.scores[step, h : h + 1, half * 128 : (half + 1) * 128] = jnp.sum(
                        lifted * attn, axis=0, keepdims=True
                    )
            return carry

        lax.fori_loop(0, STEPS, score, 0)

        def halves_max(wide):
            tile = jnp.maximum(wide[:, :128], wide[:, 128:])
            return jnp.maximum(tile, pltpu.roll(tile, 64, 1))

        def halves_sum(wide):
            return both_halves(wide[:, :128] + wide[:, 128:])

        def twice(tile):
            return jnp.concatenate([tile, tile], axis=1)

        used = [s.used[m, block, pl.ds(i, 1), :] for i in range(STEPS)]
        logits = [
            jnp.where(used[i] > 0, 0.8 * s.scores[i], -1e30) for i in range(STEPS)
        ]
        largest = twice(halves_max(functools.reduce(jnp.maximum, logits)))
        raised = [jnp.exp(logits[i] - largest) * used[i] for i in range(STEPS)]
        scale = twice(1.0 / halves_sum(functools.reduce(jnp.add, raised)))
        for i in range(STEPS):
            share = raised[i] * scale
            s.shares[p, block, i] = share
            by_head(s.low_shares, i, share.astype(BF16).astype(F32))

        def gather_head(h, carry):
            total = jnp.zeros((HEAD_WIDTH, 128), F32)
            for i in range(STEPS):
                for half in range(2):
                    lanes = pl.ds(i * LANES + half * 128, 128)
                    share = s.low_shares[h, pl.ds(i, 1), pl.ds(half * 128, 128)]
                    total = total + share * s.rows_of[p, block, head_rows(h), lanes].astype(F32)
            s.message[block, head_rows(h), :] = both_halves(total)
            return carry

        lax.fori_loop(0, HEADS, gather_head, 0)

    def normalise(p, layer, m):
        gain, shift = s.vecs[layer, 2], s.vecs[layer, 3]
        for t in range(2):
            lanes = slice(t * 128, (t + 1) * 128)
            total = jnp.where(upper_lanes(), s.message[2 * t + 1], s.message[2 * t])
            y = 2.0 * total + s.residue[m, :, lanes]
            centred = y - jnp.sum(y, axis=0, keepdims=True) * (1.0 / WIDTH)
            spread = jnp.sum(centred * centred, axis=0, keepdims=True) * (1.0 / WIDTH)
            inverse = lax.rsqrt(spread + EPSILON)
            normed = centred * inverse
            shifted = normed * gain + shift
            s.normed[p, :, lanes] = normed
            s.inverse[p, 0:1, lanes] = inverse
            act = jnp.where(shifted > 0, shifted, jnp.exp(jnp.minimum(shifted, 0.0)) - 1.0)
            s.act[:, lanes] = act.astype(BF16)

        @pl.when(p < 2)
        def _():
            s.hidden_t[p + 2] = s.act[...]
            s.hidden[p + 2] = jnp.transpose(s.act[...])
            project(p + 2, 1, m)

        @pl.when(p >= 2)
        def _():
            s.layer_output[m] = jnp.transpose(s.act[...])

    def forward(p, carry):
        m, layer = lax.rem(p, 2), lax.div(p, 2)
        if kept == 1:
            mark_big(m)
            mark_small(m)
        finish(gather_rims(p))

        def small(b, inner):
            here = pl.ds(pl.multiple_of(b * BIG, BIG), 256)
            s.turned_small[...] = jnp.transpose(s.ext[p, here])
            attend(p, layer, m, b + 1, s.turned_small, s.hot_small.at[m if kept > 1 else 0, b])

            @pl.when(b == 0)
            def _():
                finish(gather_z(p))
                start(gather_x(p))

            @pl.when(b == 1)
            def _():
                finish(gather_x(p))
                start(gather_core(p))

            return inner

        lax.fori_loop(0, 3, small, 0)
        finish(gather_core(p))

        def turn(w, inner):
            here = pl.ds(pl.multiple_of(w * 256, 256), 256)
            s.turned_big[:, here] = jnp.transpose(s.table[p, here])
            return inner

        lax.fori_loop(0, big_total // 256, turn, 0)
        attend(p, layer, m, 0, s.turned_big, s.hot_big.at[m if kept > 1 else 0])
        normalise(p, layer, m)
        return carry

    def through_norm(p, layer, m):
        gain, shift = s.vecs[layer, 2], s.vecs[layer, 3]
        for t in range(2):
            lanes = slice(t * 128, (t + 1) * 128)
            normed = s.normed[p, :, lanes]
            shifted = normed * gain + shift
            grad = s.grad_act[m, :, lanes] * jnp.where(
                shifted > 0, 1.0, jnp.exp(jnp.minimum(shifted, 0.0))
            )
            s.grad_vecs[layer, 2] = s.grad_vecs[layer, 2] + grad * normed
            s.grad_vecs[layer, 3] = s.grad_vecs[layer, 3] + grad
            grad = grad * gain
            first = jnp.sum(grad, axis=0, keepdims=True) * (1.0 / WIDTH)
            second = jnp.sum(grad * normed, axis=0, keepdims=True) * (1.0 / WIDTH)
            grad = s.inverse[p, 0:1, lanes] * (grad - first - normed * second)
            s.grad_vecs[layer, 1] = s.grad_vecs[layer, 1] + grad
            low = grad.astype(BF16)
            s.grad_out_t[p, :, lanes] = low
            wide = low.astype(F32)
            other = pltpu.roll(wide, 64, 1)
            s.grad_out[2 * t] = jnp.where(upper_lanes(), other, wide)
            s.grad_out[2 * t + 1] = jnp.where(upper_lanes(), wide, other)

    def attend_back(p, layer, block):
        s.doubled[...] = double(s.targets[p, :, tile_of(block)], block)

        def share_grads(step, carry):
            for h in range(HEADS):
                rows = slice(h * HEAD_WIDTH, (h + 1) * HEAD_WIDTH)
                grad = s.grad_out[block, rows, :]
                for half in range(2):
                    lanes = pl.ds(pl.multiple_of(step * LANES + half * 128, 128), 128)
                    got = s.rows_of[p, block, rows, lanes].astype(F32)
                    s.scores[step, h : h + 1, half * 128 : (half + 1) * 128] = jnp.sum(
                        got * grad, axis=0, keepdims=True
                    )
            return carry

        lax.fori_loop(0, STEPS, share_grads, 0)
        shares = [s.shares[p, block, i] for i in range(STEPS)]
        total = functools.reduce(jnp.add, [shares[i] * s.scores[i] for i in range(STEPS)])
        total = both_halves(total[:, :128] + total[:, 128:])
        total = jnp.concatenate([total, total], axis=1)
        for i in range(STEPS):
            by_head(s.low_shares, i, shares[i].astype(BF16).astype(F32))
            by_head(s.logit_grads, i, 0.8 * shares[i] * (s.scores[i] - total))

        def head(h, carry):
            rows = head_rows(h)
            wanted = s.doubled[rows, :]
            attn = s.vecs[layer, 0, rows, :]
            grad = s.grad_out[block, rows, :]

            target_sum = attn_sum = jnp.zeros((HEAD_WIDTH, 128), F32)
            for step in range(STEPS):
                for half in range(2):
                    lanes = pl.ds(step * LANES + half * 128, 128)
                    part = pl.ds(half * 128, 128)
                    z = s.rows_of[p, block, rows, lanes].astype(F32) + wanted
                    t = jnp.tanh(z)
                    w = t + 1.5
                    logit_grad = s.logit_grads[h, pl.ds(step, 1), part]
                    attn_sum = attn_sum + logit_grad * (z * w)
                    slope = logit_grad * (w + z * (1.0 - t * t))
                    target_sum = target_sum + slope
                    share = s.low_shares[h, pl.ds(step, 1), part]
                    s.terms[rows, lanes] = (share * grad + attn * slope).astype(BF16)
            s.grad_targets[block, rows, :] = both_halves(target_sum) * attn
            s.grad_vecs[layer, 0, rows, :] = s.grad_vecs[layer, 0, rows, :] + 2.0 * attn_sum
            return carry

        lax.fori_loop(0, HEADS, head, 0)

    def finalise(p, layer, m):
        big = reduced_unit(p)
        finish(reduce_rims(p))
        low = s.grad_small[m, pl.ds(0, RIM)] + s.land_rim[p, 0].astype(F32)
        high = s.grad_small[m, pl.ds(RIM, RIM)] + s.land_rim[p, 1].astype(F32)
        rows = jnp.concatenate([big, low, high], axis=0)
        s.grad_sources_t[p] = jnp.transpose(rows.astype(BF16))
        s.grad_act[m] = (
            nn(s.weights[layer, pl.ds(0, WIDTH)], s.grad_sources_t[p])
            + nn(s.weights[layer, pl.ds(WIDTH, WIDTH)], s.grad_targets_t[p])
            + nn(s.weights[layer, pl.ds(2 * WIDTH, WIDTH)], s.grad_out_t[p])
        )

    def weight_grads(layer):
        for k, grads in enumerate((s.grad_sources_t, s.grad_targets_t, s.grad_out_t)):
            total = nt(
                s.hidden_t[2 * layer], grads[2 * layer]
            ) + nt(s.hidden_t[2 * layer + 1], grads[2 * layer + 1])
            if shared_weights:
                s.grad_weights[pl.ds(k * WIDTH, WIDTH)] = total
            else:
                s.weight_sums[layer, pl.ds(k * WIDTH, WIDTH)] = total
        vector_rows = jnp.zeros((8, WIDTH), F32)
        for k in range(4):
            chosen = jnp.where(
                lax.broadcasted_iota(jnp.int32, (8, 128), 0) == k, 1.0, 0.0
            ).astype(F32)
            vector_rows = vector_rows + nt(
                chosen, s.grad_vecs[layer, k], precision=lax.Precision.HIGHEST
            )
        if not shared_weights:
            s.vector_sums[layer] = vector_rows
            return
        for c in range(2):
            for x in range(2):
                for z in range(depth):
                    for y in range(2):
                        chunk = ((z * 2 + x) * 2 + c) * 2 + y
                        at = (((c * 2 + x) * depth + z) * 2 + y) * 32
                        s.part[4 + layer, pl.ds(at, 32)] = jnp.concatenate(
                            [s.grad_weights[pl.ds(chunk * 24, 24)], vector_rows], axis=0
                        ).astype(BF16)
        start(reduce_core(4 + layer))

    def weight_last(layer):
        unit = reduced_unit(4 + layer)
        s.last_unit[layer] = unit
        s.last_send[layer] = unit.astype(BF16)
        start(reduce_y(layer))

    def weight_done(layer):
        finish(reduce_y(layer))
        mine = s.last_unit[layer, pl.ds(pl.multiple_of(own_f * 32, 32), 32)]
        total = mine + s.land_y[layer].astype(F32)
        s.weight_sums[layer] = total[:24]
        s.vector_sums[layer] = total[24:]

    def backward(i, carry):
        p = lax.rem(i + 2, 4)
        m, layer = lax.rem(p, 2), lax.div(p, 2)
        if kept == 1:
            mark_big(m)
            mark_small(m)

        @pl.when(i >= 2)
        def _():
            finalise(p + 2, 1, m)

        @pl.when(i == 3)
        def _():
            weight_grads(1)

        through_norm(p, layer, m)
        attend_back(p, layer, 0)

        def scatter_big(w, inner):
            here = pl.ds(pl.multiple_of(w * 256, 256), 256)
            slot = m if kept > 1 else 0
            s.part[p, here] = nt(s.hot_big[slot, here], s.terms[...]).astype(BF16)
            return inner

        lax.fori_loop(0, big_total // 256, scatter_big, 0)
        start(reduce_core(p))
        s.grad_ext[...] = jnp.zeros_like(s.grad_ext)

        def small(b, inner):
            attend_back(p, layer, b + 1)
            here = pl.ds(pl.multiple_of(b * BIG, BIG), 256)
            s.grad_ext[here] = s.grad_ext[here] + nt(s.hot_small[m if kept > 1 else 0, b], s.terms[...])

            @pl.when(b == 0)
            def _():
                reduce_to_x(p)
                if shared_weights:

                    @pl.when(i == 3)
                    def _():
                        reduce_to_x(5)

            @pl.when(b == 1)
            def _():
                reduce_to_z(p)
                if shared_weights:

                    @pl.when(i == 3)
                    def _():
                        reduce_to_z(5)

            return inner

        lax.fori_loop(0, 3, small, 0)
        s.send_rim[p, 0] = s.grad_ext[pl.ds(0, RIM)].astype(BF16)
        s.send_rim[p, 1] = s.grad_ext[pl.ds(RIM + SMALL, RIM)].astype(BF16)
        start(reduce_rims(p))
        s.grad_small[m] = s.grad_ext[pl.ds(RIM, SMALL)]
        for t in range(2):
            lanes = slice(t * 128, (t + 1) * 128)
            s.grad_targets_t[p, :, lanes] = jnp.where(
                upper_lanes(), s.grad_targets[2 * t + 1], s.grad_targets[2 * t]
            ).astype(BF16)
        return carry

    barrier = pltpu.get_barrier_semaphore()
    partners = [dict(blk=d) for d in [*z_peers, x_peer, sibling, before, after]]
    if shared_weights:
        partners.append(dict(fsdp=1 - own_f))
    for partner in partners:
        pl.semaphore_signal(barrier, inc=1, device_id=partner, device_id_type=MESH)
    pl.semaphore_wait(barrier, len(partners))

    if shared_weights:
        for layer in range(LAYERS):
            s.table[4 + layer, pl.ds(pl.multiple_of(own_row + own_f * 32, 32), 32)] = (
                s.weight_units[layer]
            )
            start(gather_y(4 + layer))
    prepare(0)
    prepare(1)
    s.scores[...] = jnp.zeros_like(s.scores)
    s.grad_vecs[...] = jnp.zeros_like(s.grad_vecs)
    if shared_weights:
        for layer in range(LAYERS):
            finish(gather_y(4 + layer))
            start(gather_z(4 + layer))
    if kept > 1:
        mark_small(0)
    if shared_weights:
        for layer in range(LAYERS):
            finish(gather_z(4 + layer))
            start(gather_x(4 + layer))
    if kept > 1:
        mark_small(1)
    if shared_weights:
        for layer in range(LAYERS):
            finish(gather_x(4 + layer))
            start(gather_core(4 + layer))
    if kept > 1:
        mark_big(0)
        mark_big(1)
    if shared_weights:
        finish(gather_core(4))
    load_layer(0)
    project(0, 0, 0)
    project(1, 0, 1)
    if shared_weights:
        finish(gather_core(5))
    load_layer(1)
    lax.fori_loop(0, 4, forward, 0)
    lax.fori_loop(0, 4, backward, 0)
    if shared_weights:
        weight_last(1)
    finalise(0, 0, 0)
    s.input_gradient[0] = jnp.transpose(s.grad_act[0])
    finalise(1, 0, 1)
    weight_grads(0)
    s.input_gradient[1] = jnp.transpose(s.grad_act[1])
    if shared_weights:
        reduce_to_x(4)
        weight_done(1)
        reduce_to_z(4)
        weight_last(0)
        weight_done(0)


def per_device(depth, fsdp_count, features, neighbours, slot_mask, projections, vectors, out_cotangent):
    layers, weight_chunk = projections.shape
    vector_chunk = vectors.shape[1]
    place = lax.axis_index("blk") * fsdp_count + lax.axis_index("fsdp")
    shared_weights = fsdp_count == 2 and weight_chunk == 24 * WIDTH and depth == 4
    inputs = dict(
        features=features[:, 0],
        neighbours=neighbours[:, 0],
        slot_mask=slot_mask[:, 0],
        out_cotangent=out_cotangent[:, 0],
    )
    if shared_weights:
        own = lax.dynamic_update_slice(
            jnp.zeros((layers, 8 * WIDTH), BF16), vectors, (0, place * vector_chunk)
        )
        inputs["weight_units"] = jnp.concatenate(
            [projections.reshape(layers, 24, WIDTH), own.reshape(layers, 8, WIDTH)], axis=1
        )
        weight_rows = 24
    else:
        axes = ("blk", "fsdp")
        gathered = lax.all_gather(projections, axes, axis=1, tiled=True)
        inputs["weights"] = gathered.reshape(layers, 3 * WIDTH, WIDTH)
        gathered = lax.all_gather(vectors, axes, axis=1, tiled=True)
        inputs["all_vectors"] = jnp.pad(
            gathered.reshape(layers, 4, WIDTH), ((0, 0), (0, 4), (0, 0))
        )
        weight_rows = 3 * WIDTH
    outputs = dict(
        layer_output=jax.ShapeDtypeStruct((MICRO, NODES, WIDTH), BF16),
        input_gradient=jax.ShapeDtypeStruct((MICRO, NODES, WIDTH), F32),
        weight_sums=jax.ShapeDtypeStruct((layers, weight_rows, WIDTH), F32),
        vector_sums=jax.ShapeDtypeStruct((layers, 8, WIDTH), F32),
    )
    scratch = scratch_plan(depth, shared_weights)
    in_vmem = pl.BlockSpec(memory_space=pltpu.VMEM)
    layer_output, input_gradient, weight_sums, vector_sums = pl.pallas_call(
        functools.partial(
            step_kernel, depth, shared_weights, [*inputs, *outputs, *scratch]
        ),
        out_shape=list(outputs.values()),
        in_specs=[in_vmem] * len(inputs),
        out_specs=[in_vmem] * len(outputs),
        scratch_shapes=list(scratch.values()),
        compiler_params=pltpu.CompilerParams(
            collective_id=0, has_side_effects=True, vmem_limit_bytes=63 * 1024 * 1024
        ),
    )(*inputs.values())
    if shared_weights:
        weight_sums = weight_sums.reshape(layers, weight_chunk)
        vector_sums = lax.dynamic_slice(
            vector_sums.reshape(layers, 8 * WIDTH),
            (0, place * vector_chunk),
            (layers, vector_chunk),
        )
    else:
        axes = ("blk", "fsdp")
        weight_sums = lax.psum_scatter(
            weight_sums.reshape(layers, -1), axes, scatter_dimension=1, tiled=True
        )
        vector_sums = lax.psum_scatter(
            vector_sums[:, :4].reshape(layers, -1), axes, scatter_dimension=1, tiled=True
        )
    return layer_output[:, None], input_gradient[:, None], weight_sums, vector_sums


def solution(mesh):
    return jax.shard_map(
        functools.partial(per_device, mesh.shape["blk"] // 4, mesh.shape["fsdp"]),
        mesh=mesh,
        in_specs=(
            P(None, "fsdp", "blk", None),
            P(None, "fsdp", "blk", None),
            P(None, "fsdp", "blk", None),
            P(None, ("blk", "fsdp")),
            P(None, ("blk", "fsdp")),
            P(None, "fsdp", "blk", None),
        ),
        out_specs=(
            P(None, "fsdp", "blk", None),
            P(None, "fsdp", "blk", None),
            P(None, ("blk", "fsdp")),
            P(None, ("blk", "fsdp")),
        ),
        check_vma=False,
    )
```

time: 1230 us -> 169 us (0.14)
  local copies, waits for them, and re-layouts: 393 us -> 7.93 us
  waiting for transfers between devices: 240 us -> 0 us
  blocking collectives: 223 us -> 0 us
  other arithmetic: 213 us -> 0.62 us
  Pallas kernels: 0 us -> 160 us
  matrix products: 133 us -> 0 us
  between operations: 16.5 us -> 0.72 us
    pallas_call x0 -> x1, Pallas kernels: none -> 160 us  [per_device(): pl.pallas_call(functools.partial(step_kernel, depth, shared_weights, [*in...]
    all_gather x2 -> x0, blocking collectives: 145 us -> none  [fetch(): lax.all_gather(projections[layer_index], ('blk', 'fsdp'), axis=0, tiled=T...]
    slice x54 -> x0, local copies, waits for them, and re-layouts: 138 us -> none  [the longest x8 62.9 us: per_device(): backward_grad_gathered[quarter:].reshape(-1, feature_width)]
    dot_general x48 -> x0, matrix products: 133 us -> none  [the longest x8 34.4 us: pick_rows(): jnp.dot(selector, table, preferred_element_type=jnp.float32)]
    unnamed x10 -> x0, waiting for transfers between devices: 132 us -> none
    concatenate x16 -> x0, local copies, waits for them, and re-layouts: 99.7 us -> none  [take_sources(): return jnp.concatenate([big_rows, small_part], axis=0)]
    unnamed x2 -> x0, blocking collectives: 77.7 us -> none
    reduce_scatter x4 -> x0, waiting for transfers between devices: 69.4 us -> none  [per_device(): lax.psum_scatter(full_terms.astype(jnp.bfloat16), 'blk', scatter_dimensio...]
  transfers between devices with their start and end apart: 9 -> 0, of which waited for: 5 -> 0; matrix products, arithmetic and copies ran while one was open for 17% -> 0% of each run, Pallas kernels for 0% -> 0%
where the time goes in v1:
time: 169 us
  Pallas kernels  160 us (95%)
  local copies, waits for them, and re-layouts  7.93 us (5%)
    pallas_call x1, Pallas kernels, per_device(): pl.pallas_call(functools.partial(step_kernel, depth, shared_weights, [*in...  160 us
    unnamed x18, local copies, waits for them, and re-layouts  7.2 us

profile of v1, /device:TPU:0, one launch (start us, length us, event | category | flops | bytes accessed | tf_op | source)
XLA Modules:
  0.0 168.9 jit_solution(3491150647813213737)
XLA Ops:
  0.6 0.0 copy-start.3
  0.6 0.0 copy-start.4
  0.7 0.6 copy-done.4
  1.3 0.1 dynamic_update_slice.3
  1.4 0.0 copy-start.1
  1.4 0.0 copy-done.3
  1.4 0.6 pad_maximum_fusion.refs_4_
  2.1 0.2 copy-done.1
  2.2 0.0 copy-start.2
  2.2 0.8 copy.10
  3.1 0.0 copy-done.2
  3.1 0.8 copy.11
  3.9 159.6 %shard_map.93 = (bf16[2,256,256]{2,1,0:T(8,128)(2,1)}, f32[2,256,256]{2,1,0:T(8,128)}, f32[2,24,256]{2,1,0:T(8,128)}, f32[2,8,256]{2,1,0:T(8,128)}) custom-call(bf16[2,256,256]{2,1,0:T(8,128)(2,1)} %bitcast.26, s32[2,256,32]{2,1,0:T(8,128)} %bitcast.22, s32[2,256,32]{2,1,0:T(8,128)} %bitcast.23, bf16[2,256,256]{2,1,0:T(8,128)(2,1)} %bitcast.27, ...), custom_call_target="tpu_custom_call" | custom-call | tf_op jit(solution)/shard_map/pallas_call | solution.py:806
  163.5 0.0 copy-start
  163.6 0.8 copy.17
  164.3 0.6 constant_dynamic-slice_fusion
  165.0 1.4 copy.16
  166.4 1.7 copy.25
  168.1 0.0 copy-done
  168.1 0.8 copy.26
  (3 shorter events, 0.0 us)
Async XLA Ops:
  0.6 0.8 copy-start.3
  0.6 0.7 copy-start.4
  1.4 0.8 copy-start.1
  2.2 0.8 copy-start.2
  163.5 4.6 %copy-start = (f32[2,256,256]{2,1,0:T(8,128)S(1)}, f32[2,256,256]{2,1,0:T(8,128)}, u32[]{:S(2)}) copy-start(f32[2,256,256]{2,1,0:T(8,128)} %get-tuple-element.9) | copy-start | bytes 1572868

commit v2 on v1

v2 whole, which is shorter than its diff:
```python
import functools
import types

import jax
import jax.numpy as jnp
from jax import lax
from jax.experimental import pallas as pl
from jax.experimental.pallas import tpu as pltpu
from jax.sharding import PartitionSpec as P

HEADS = 4
MICRO = 2
LAYERS = 2
SLOTS = 32
WIDTH = 256
HEAD_WIDTH = WIDTH // HEADS
NODES = 256
BIG = 64
SMALL = NODES - BIG
RIM = 96
EXT = SMALL + 2 * RIM
BLOCKS = NODES // BIG
SMALLS = BLOCKS - 1
PAIRS = BIG * SLOTS
STEPS = 8
LANES = PAIRS // STEPS
UNIT = BIG
CHUNK = 24
PIECE = UNIT // 2
EPSILON = 1e-05
F32 = jnp.float32
BF16 = jnp.bfloat16
MESH = pl.DeviceIdType.MESH


def nn(left, right):
    return lax.dot_general(
        left, right, (((1,), (0,)), ((), ())), preferred_element_type=F32
    )


def nt(left, right, precision=None):
    return lax.dot_general(
        left, right, (((1,), (1,)), ((), ())), preferred_element_type=F32, precision=precision
    )


def tn(left, right):
    return lax.dot_general(
        left, right, (((0,), (0,)), ((), ())), preferred_element_type=F32
    )


def upper_lanes():
    return lax.broadcasted_iota(jnp.int32, (WIDTH, 128), 1) >= 64


def join_halves(even, odd):
    upper = upper_lanes()
    return jnp.where(upper, odd, even) + pltpu.roll(jnp.where(upper, even, odd), 64, 1)


def scratch_plan(depth, shared_weights):
    big_total = 4 * depth * UNIT
    tables = 4 + (LAYERS if shared_weights else 0)
    copies = MICRO if depth <= 4 else 1
    peers = 2 * depth - 1
    vm = pltpu.VMEM
    plan = dict(
        hot_big=vm((copies, big_total, PAIRS), BF16),
        hot_small=vm((copies, SMALLS, 256, PAIRS), BF16),
        place=vm((MICRO, BLOCKS, STEPS, LANES), jnp.int32),
        used=vm((MICRO, BLOCKS, STEPS, LANES), F32),
        rows_0=vm((4, WIDTH, PAIRS), BF16),
        rows_1=vm((4, WIDTH, PAIRS), BF16),
        rows_2=vm((4, WIDTH, PAIRS), BF16),
        rows_3=vm((4, WIDTH, PAIRS), BF16),
        shares=vm((4, BLOCKS, STEPS, 8, LANES), F32),
        table=vm((tables, big_total, WIDTH), BF16),
        ext=vm((4, EXT, WIDTH), BF16),
        turned_big=vm((WIDTH, big_total), BF16),
        turned_small=vm((SMALLS, WIDTH, 256), BF16),
        hidden_t=vm((4, WIDTH, NODES), BF16),
        weights_t=vm((LAYERS, 2 * WIDTH, WIDTH), BF16),
        vecs=vm((LAYERS, 4, WIDTH, 128), F32),
        attn_low=vm((LAYERS, WIDTH, 128), BF16),
        targets=vm((4, WIDTH, NODES), F32),
        residue=vm((MICRO, WIDTH, NODES), F32),
        doubled=vm((BLOCKS, WIDTH, 128), F32),
        doubled_low=vm((BLOCKS, WIDTH, 128), BF16),
        scores=vm((BLOCKS, STEPS, 8, LANES), F32),
        message=vm((MICRO, BLOCKS, WIDTH, 128), F32),
        normed=vm((4, WIDTH, NODES), F32),
        inverse=vm((4, 8, NODES), F32),
        act=vm((WIDTH, NODES), BF16),
        grad_act=vm((MICRO, WIDTH, NODES), F32),
        grad_out=vm((MICRO, BLOCKS, WIDTH, 128), BF16),
        grad_out_t=vm((4, WIDTH, NODES), BF16),
        grad_targets_t=vm((4, WIDTH, NODES), BF16),
        grad_sources_t=vm((4, WIDTH, NODES), BF16),
        terms_0=vm((WIDTH, PAIRS), BF16),
        terms_1=vm((WIDTH, PAIRS), BF16),
        grad_ext=vm((EXT, WIDTH), F32),
        grad_small=vm((MICRO, SMALL, WIDTH), F32),
        grad_vecs=vm((LAYERS, 4, WIDTH, 128), F32),
        land_core=vm((tables, big_total // 2, WIDTH), BF16),
        land=vm((4, peers, UNIT, WIDTH), BF16),
        land_rim=vm((4, 2, RIM, WIDTH), BF16),
        send_rim=vm((4, 2, RIM, WIDTH), BF16),
        gather_send=pltpu.SemaphoreType.DMA((tables, 18)),
        gather_recv=pltpu.SemaphoreType.DMA((tables, 18)),
        reduce_send=pltpu.SemaphoreType.DMA((tables, 18)),
        reduce_recv=pltpu.SemaphoreType.DMA((tables, 18)),
    )
    if shared_weights:
        plan.update(
            weights=vm((LAYERS, 3 * WIDTH, WIDTH), BF16),
            grad_weights=vm((3 * WIDTH, WIDTH), F32),
            land_piece=vm((LAYERS, 2 * peers + 1, PIECE, WIDTH), BF16),
        )
    return plan


def step_kernel(depth, shared_weights, names, *refs):
    s = types.SimpleNamespace(**dict(zip(names, refs, strict=True)))
    big_total = 4 * depth * UNIT
    kept = s.hot_big.shape[0]
    me = lax.axis_index("blk")
    core = lax.rem(me, 2)
    along_x = lax.rem(lax.div(me, 2), 2)
    along_z = lax.div(me, 4)
    own_f = lax.axis_index("fsdp")
    block_count = 4 * depth
    before = lax.rem(me + block_count - 1, block_count)
    after = lax.rem(me + 1, block_count)
    sibling = along_z * 4 + along_x * 2 + (1 - core)

    def unit_row(z, x, c):
        return pl.multiple_of(((c * 2 + x) * depth + z) * UNIT, UNIT)

    own_row = unit_row(along_z, along_x, core)
    rows_of = (s.rows_0, s.rows_1, s.rows_2, s.rows_3)
    terms = (s.terms_0, s.terms_1)
    far = []
    for dz in sorted(range(depth), reverse=True):
        for dx in (1, 0):
            if dz or dx:
                z, x = lax.rem(along_z + dz, depth), lax.rem(along_x + dx, 2)
                far.append((z * 4 + x * 2 + core, unit_row(z, x, core)))

    def remote(src, dst, sems, slot, **where):
        send, recv = sems
        return pltpu.make_async_remote_copy(
            src_ref=src,
            dst_ref=dst,
            send_sem=send.at[slot],
            recv_sem=recv.at[slot],
            device_id=where,
            device_id_type=MESH,
        )

    gather_sems = (s.gather_send, s.gather_recv)
    reduce_sems = (s.reduce_send, s.reduce_recv)
    core_slot, low_slot, high_slot = 15, 16, 17

    def half_rows(c):
        return pl.ds(unit_row(0, 0, c), 2 * depth * UNIT)

    def piece_rows(row, f):
        return pl.ds(pl.multiple_of(row + f * PIECE, PIECE), PIECE)

    def gather_far(p):
        unit = s.table.at[p, pl.ds(own_row, UNIT)]
        return [
            remote(unit, unit, gather_sems, (p, k), blk=peer)
            for k, (peer, _) in enumerate(far)
        ]

    def all_far():
        found = []
        for peer, row in far:
            for f in (1 - own_f, own_f):
                found.append((peer, f, piece_rows(row, f)))
        found.append((me, 1 - own_f, piece_rows(own_row, 1 - own_f)))
        return found

    def gather_pieces(layer):
        piece = s.table.at[4 + layer, piece_rows(own_row, own_f)]
        return [
            remote(piece, piece, gather_sems, (4 + layer, k), blk=peer, fsdp=f)
            for k, (peer, f, _) in enumerate(all_far())
        ]

    def gather_core(q):
        half = s.table.at[q, half_rows(core)]
        return [remote(half, half, gather_sems, (q, core_slot), blk=sibling)]

    def gather_rims(p):
        low = remote(
            s.ext.at[p, pl.ds(RIM, RIM)],
            s.ext.at[p, pl.ds(RIM + SMALL, RIM)],
            gather_sems,
            (p, low_slot),
            blk=before,
        )
        high = remote(
            s.ext.at[p, pl.ds(SMALL, RIM)],
            s.ext.at[p, pl.ds(0, RIM)],
            gather_sems,
            (p, high_slot),
            blk=after,
        )
        return [low, high]

    def reduce_core(q):
        return [
            remote(
                s.table.at[q, half_rows(1 - core)],
                s.land_core.at[q],
                reduce_sems,
                (q, core_slot),
                blk=sibling,
            )
        ]

    def reduce_far(p):
        return [
            remote(
                s.table.at[p, pl.ds(row, UNIT)],
                s.land.at[p, k],
                reduce_sems,
                (p, k),
                blk=peer,
            )
            for k, (peer, row) in enumerate(far)
        ]

    def reduce_pieces(layer):
        return [
            remote(
                s.table.at[4 + layer, rows],
                s.land_piece.at[layer, k],
                reduce_sems,
                (4 + layer, k),
                blk=peer,
                fsdp=f,
            )
            for k, (peer, f, rows) in enumerate(all_far())
        ]

    def reduce_rims(p):
        low = remote(
            s.send_rim.at[p, 0], s.land_rim.at[p, 1], reduce_sems, (p, low_slot), blk=before
        )
        high = remote(
            s.send_rim.at[p, 1], s.land_rim.at[p, 0], reduce_sems, (p, high_slot), blk=after
        )
        return [low, high]

    def start(copies):
        for copy in copies:
            copy.start()

    def finish(copies):
        for copy in copies:
            copy.wait()

    def add_core(q):
        finish(reduce_core(q))
        first = unit_row(0, 0, core)

        def body(i, carry):
            here = pl.ds(pl.multiple_of(first + i * UNIT, UNIT), UNIT)
            there = pl.ds(pl.multiple_of(i * UNIT, UNIT), UNIT)
            s.table[q, here] = (
                s.table[q, here].astype(F32) + s.land_core[q, there].astype(F32)
            ).astype(BF16)
            return carry

        lax.fori_loop(0, 2 * depth, body, 0)

    def reduce_on(p):
        add_core(p)
        start(reduce_far(p))

    def reduced_unit(p):
        finish(reduce_far(p))
        total = s.table[p, pl.ds(own_row, UNIT)].astype(F32)
        for k in range(len(far)):
            total = total + s.land[p, k].astype(F32)
        return total

    def prepare(m):
        def compact(rows, block):
            part = rows[:, block * BIG : (block + 1) * BIG]
            tile = jnp.concatenate([part[:16], part[16:]], axis=1)
            return jnp.concatenate([tile[:8], tile[8:]], axis=1)

        picked = s.neighbours[m]
        usable = s.slot_mask[m]
        device = lax.shift_right_logical(picked, 8)
        offset = jnp.bitwise_and(picked, 255)
        z = lax.shift_right_logical(device, 2)
        x = jnp.bitwise_and(lax.shift_right_logical(device, 1), 1)
        c = jnp.bitwise_and(device, 1)
        big_place = ((c * 2 + x) * depth + z) * UNIT + offset
        small_place = (device - me) * SMALL + (offset - BIG)
        for block in range(BLOCKS):
            if block == 0:
                s.place[m, 0] = compact(big_place, 0)
            else:
                s.place[m, block] = compact(small_place + (RIM - (block - 1) * BIG), block)
            s.used[m, block] = compact(usable, block).astype(F32)
        s.hidden_t[m] = jnp.transpose(s.features[m])
        s.grad_act[m] = jnp.transpose(s.out_cotangent[m].astype(F32))

    def mark(row, least):
        tile = lax.broadcasted_iota(jnp.int32, (256, LANES), 0)
        return jnp.where(tile == row - least, 1.0, 0.0).astype(BF16)

    def lanes_of(step):
        return pl.ds(pl.multiple_of(step * LANES, LANES), LANES)

    def mark_big(m):
        slot = m if kept > 1 else 0

        def tile(w, carry):
            here = pl.ds(pl.multiple_of(w * 256, 256), 256)
            for step in range(STEPS):
                lanes = pl.ds(step * LANES, LANES)
                row = s.place[m, 0, pl.ds(step, 1), :]
                s.hot_big[slot, here, lanes] = mark(row, w * 256)
            return carry

        lax.fori_loop(0, big_total // 256, tile, 0)

    def mark_small(m):
        slot = m if kept > 1 else 0

        def block_body(b, carry):
            for step in range(STEPS):
                lanes = pl.ds(step * LANES, LANES)
                row = s.place[m, b + 1, pl.ds(step, 1), :]
                s.hot_small[slot, b, :, lanes] = mark(row, 0)
            return carry

        lax.fori_loop(0, SMALLS, block_body, 0)

    place = me * 2 + own_f
    vector_row, vector_lane = lax.div(place, 8), lax.rem(place, 8) * 32

    def vector_place():
        lane = lax.broadcasted_iota(jnp.int32, (32, WIDTH), 1)
        element = lax.broadcasted_iota(jnp.int32, (32, WIDTH), 0)
        return jnp.where(lane == element + vector_lane, 1.0, 0.0)

    def own_row_of_eight():
        return lax.broadcasted_iota(jnp.int32, (8, WIDTH), 0) == vector_row

    def own_piece(layer):
        flat = s.projections[...].astype(F32)[layer : layer + 1]
        rows = [flat[:, i * WIDTH : (i + 1) * WIDTH] for i in range(CHUNK)]
        own = s.vectors[...][layer : layer + 1].astype(F32)
        own = nn(jnp.broadcast_to(own, (8, 32)).astype(BF16), vector_place().astype(BF16))
        rows.append(jnp.where(own_row_of_eight(), own, 0.0))
        s.table[4 + layer, piece_rows(own_row, own_f)] = jnp.concatenate(
            rows, axis=0
        ).astype(BF16)

    def chunks():
        for c in range(2):
            for x in range(2):
                for z in range(depth):
                    for y in range(2):
                        yield (
                            ((z * 2 + x) * 2 + c) * 2 + y,
                            (((c * 2 + x) * depth + z) * 2 + y) * PIECE,
                        )

    def load_layer(layer):
        if shared_weights:
            pieces = {
                chunk: s.table[4 + layer, pl.ds(at, PIECE)].astype(F32)
                for chunk, at in chunks()
            }
            s.weights[layer] = jnp.concatenate(
                [pieces[i][:CHUNK] for i in range(len(pieces))], axis=0
            ).astype(BF16)
            rows = pieces[0][CHUNK:]
            for i in range(1, len(pieces)):
                rows = rows + pieces[i][CHUNK:]
        else:
            rows = s.all_vectors[layer].astype(F32)
        for k in range(2):
            s.weights_t[layer, pl.ds(k * WIDTH, WIDTH)] = jnp.transpose(
                s.weights[layer, pl.ds((k + 1) * WIDTH, WIDTH)]
            )
        which = lax.broadcasted_iota(jnp.int32, (8, 512), 0)
        lane = lax.shift_right_logical(lax.broadcasted_iota(jnp.int32, (8, 512), 1), 7)
        chosen = jnp.where(which == lane, 1.0, 0.0).astype(BF16)
        wide = tn(rows.astype(BF16), chosen)
        for k in range(4):
            s.vecs[layer, k] = wide[:, k * 128 : (k + 1) * 128]
        s.attn_low[layer] = wide[:, :128].astype(BF16)

    def project(p, layer, m, hidden):
        sources = (0.5 * nn(hidden, s.weights[layer, pl.ds(0, WIDTH)])).astype(BF16)
        s.table[p, pl.ds(own_row, UNIT)] = sources[:BIG]
        s.ext[p, pl.ds(RIM, SMALL)] = sources[BIG:]
        start(gather_rims(p))
        start(gather_far(p))
        s.targets[p] = 0.5 * nt(s.weights_t[layer, pl.ds(0, WIDTH)], hidden)
        bias = s.vecs[layer, 1]
        s.residue[m] = nt(s.weights_t[layer, pl.ds(WIDTH, WIDTH)], hidden) + jnp.concatenate(
            [bias, bias], axis=1
        )

    def spread(p, block, low):
        wide = s.targets[p, :, pl.ds((block // 2) * 128, 128)]
        odd = block % 2 == 1
        tile = jnp.where(upper_lanes() == odd, wide, pltpu.roll(wide, 64, 1))
        if low:
            s.doubled_low[block] = tile.astype(BF16)
        else:
            s.doubled[block] = tile

    def score(p, layer, block, step):
        for h in range(HEADS):
            rows = slice(h * HEAD_WIDTH, (h + 1) * HEAD_WIDTH)
            wanted = s.doubled[block, rows, :]
            attn = s.vecs[layer, 0, rows, :]
            for half in range(2):
                lanes = pl.ds(pl.multiple_of(step * LANES + half * 128, 128), 128)
                z = rows_of[block][p, rows, lanes].astype(F32) + wanted
                lifted = z * (jnp.tanh(z) + 1.5)
                s.scores[block, step, h : h + 1, half * 128 : (half + 1) * 128] = jnp.sum(
                    lifted * attn, axis=0, keepdims=True
                )

    def halves_max(wide):
        tile = jnp.maximum(wide[:, :128], wide[:, 128:])
        tile = jnp.maximum(tile, pltpu.roll(tile, 64, 1))
        return jnp.concatenate([tile, tile], axis=1)

    def halves_sum(wide):
        tile = wide[:, :128] + wide[:, 128:]
        tile = tile + pltpu.roll(tile, 64, 1)
        return jnp.concatenate([tile, tile], axis=1)

    def softmax(p, m, blocks):
        for block in blocks:
            used = [s.used[m, block, pl.ds(i, 1), :] for i in range(STEPS)]
            logits = [
                jnp.where(used[i] > 0, 0.8 * s.scores[block, i], -1e30) for i in range(STEPS)
            ]
            largest = halves_max(functools.reduce(jnp.maximum, logits))
            raised = [jnp.exp(logits[i] - largest) * used[i] for i in range(STEPS)]
            scale = 1.0 / halves_sum(functools.reduce(jnp.add, raised))
            for i in range(STEPS):
                share = raised[i] * scale
                s.shares[p, block, i] = share

    def pass_message(p, m, block, step):
        for h in range(HEADS):
            rows = slice(h * HEAD_WIDTH, (h + 1) * HEAD_WIDTH)
            total = s.message[m, block, rows, :]
            for half in range(2):
                lanes = pl.ds(pl.multiple_of(step * LANES + half * 128, 128), 128)
                share = s.shares[p, block, step, h : h + 1, half * 128 : (half + 1) * 128]
                share = share.astype(BF16).astype(F32)
                total = total + share * rows_of[block][p, rows, lanes].astype(F32)
            s.message[m, block, rows, :] = total

    def small_rows(p, m, b, part):
        lanes = pl.ds(part * 2 * LANES, 2 * LANES)
        hot = s.hot_small[m if kept > 1 else 0, b, :, lanes]
        rows_of[b + 1][p, :, lanes] = nn(s.turned_small[b], hot).astype(BF16)

    def big_rows(p, m, part):
        lanes = pl.ds(part * 2 * LANES, 2 * LANES)
        hot = s.hot_big[m if kept > 1 else 0, :, lanes]
        rows_of[0][p, :, lanes] = nn(s.turned_big[...], hot).astype(BF16)

    def smalls(p, layer, m):
        finish(gather_rims(p))
        for b in range(SMALLS):
            s.turned_small[b] = jnp.transpose(s.ext[p, pl.ds(b * BIG, 256)])
            spread(p, b + 1, False)
        for part in range(STEPS // 2):
            small_rows(p, m, 0, part)
        for b in range(SMALLS):
            for step in range(STEPS):
                score(p, layer, b + 1, step)
                if b + 1 < SMALLS and step % 2:
                    small_rows(p, m, b + 1, step // 2)

    def big(p, layer, m):
        def turn(w, inner):
            here = pl.ds(pl.multiple_of(w * 256, 256), 256)
            s.turned_big[:, here] = jnp.transpose(s.table[p, here])
            return inner

        lax.fori_loop(0, big_total // 256, turn, 0)
        spread(p, 0, False)
        s.message[m] = jnp.zeros((BLOCKS, WIDTH, 128), F32)

        for part in range(STEPS // 2):
            big_rows(p, m, part)
            for block in range(1, BLOCKS):
                for step in (2 * part, 2 * part + 1):
                    pass_message(p, m, block, step)

        def body(step, carry):
            score(p, layer, 0, step)
            return carry

        lax.fori_loop(0, STEPS, body, 0)
        softmax(p, m, [0])

        def message_body(step, carry):
            pass_message(p, m, 0, step)
            return carry

        lax.fori_loop(0, STEPS, message_body, 0)

    def normalise(p, layer, m):
        gain, shift = s.vecs[layer, 2], s.vecs[layer, 3]
        for t in range(2):
            lanes = slice(t * 128, (t + 1) * 128)
            total = join_halves(s.message[m, 2 * t], s.message[m, 2 * t + 1])
            y = 2.0 * total + s.residue[m, :, lanes]
            centred = y - jnp.sum(y, axis=0, keepdims=True) * (1.0 / WIDTH)
            spread_of = jnp.sum(centred * centred, axis=0, keepdims=True) * (1.0 / WIDTH)
            inverse = lax.rsqrt(spread_of + EPSILON)
            normed = centred * inverse
            shifted = normed * gain + shift
            s.normed[p, :, lanes] = normed
            s.inverse[p, 0:1, lanes] = inverse
            act = jnp.where(shifted > 0, shifted, jnp.exp(jnp.minimum(shifted, 0.0)) - 1.0)
            s.act[:, lanes] = act.astype(BF16)

        @pl.when(layer == 0)
        def _():
            s.hidden_t[m + 2] = s.act[...]
            project(m + 2, 1, m, jnp.transpose(s.act[...]))

        @pl.when(layer == 1)
        def _():
            s.layer_output[m] = jnp.transpose(s.act[...])

    def forward(layer, carry):
        first, second = 2 * layer, 2 * layer + 1

        def small_body(m, inner):
            if kept == 1:
                mark_small(m)
            smalls(first + m, layer, m)

            @pl.when(m == 1)
            def _():
                finish(gather_far(first))
                start(gather_core(first))

            softmax(first + m, m, [1, 2, 3])
            return inner

        lax.fori_loop(0, MICRO, small_body, 0)

        def big_body(m, inner):
            if kept == 1:
                mark_big(m)
            finish(gather_core(first + m))
            big(first + m, layer, m)

            @pl.when(m == 0)
            def _():
                finish(gather_far(second))
                start(gather_core(second))

            normalise(first + m, layer, m)
            return inner

        lax.fori_loop(0, MICRO, big_body, 0)
        return carry

    def through_norm(p, layer, m):
        gain, shift = s.vecs[layer, 2], s.vecs[layer, 3]
        upper = upper_lanes()
        for t in range(2):
            lanes = slice(t * 128, (t + 1) * 128)
            normed = s.normed[p, :, lanes]
            shifted = normed * gain + shift
            grad = s.grad_act[m, :, lanes] * jnp.where(
                shifted > 0, 1.0, jnp.exp(jnp.minimum(shifted, 0.0))
            )
            s.grad_vecs[layer, 2] = s.grad_vecs[layer, 2] + grad * normed
            s.grad_vecs[layer, 3] = s.grad_vecs[layer, 3] + grad
            grad = grad * gain
            first = jnp.sum(grad, axis=0, keepdims=True) * (1.0 / WIDTH)
            second = jnp.sum(grad * normed, axis=0, keepdims=True) * (1.0 / WIDTH)
            grad = s.inverse[p, 0:1, lanes] * (grad - first - normed * second)
            s.grad_vecs[layer, 1] = s.grad_vecs[layer, 1] + grad
            s.grad_out_t[p, :, lanes] = grad.astype(BF16)
            other = pltpu.roll(grad, 64, 1)
            s.grad_out[m, 2 * t] = jnp.where(upper, other, grad).astype(BF16)
            s.grad_out[m, 2 * t + 1] = jnp.where(upper, grad, other).astype(BF16)

    def share_grads(p, m, block, step):
        for h in range(HEADS):
            rows = slice(h * HEAD_WIDTH, (h + 1) * HEAD_WIDTH)
            grad = s.grad_out[m, block, rows, :]
            for half in range(2):
                lanes = pl.ds(pl.multiple_of(step * LANES + half * 128, 128), 128)
                product = rows_of[block][p, rows, lanes] * grad
                s.scores[block, step, h : h + 1, half * 128 : (half + 1) * 128] = jnp.sum(
                    product.astype(F32), axis=0, keepdims=True
                )

    def logit_grads(p, blocks):
        for block in blocks:
            shares = [s.shares[p, block, i] for i in range(STEPS)]
            total = halves_sum(
                functools.reduce(
                    jnp.add, [shares[i] * s.scores[block, i] for i in range(STEPS)]
                )
            )
            for i in range(STEPS):
                s.scores[block, i] = 0.8 * shares[i] * (s.scores[block, i] - total)

    def make_terms(p, layer, m, block, step):
        for h in range(HEADS):
            rows = slice(h * HEAD_WIDTH, (h + 1) * HEAD_WIDTH)
            wanted = s.doubled_low[block, rows, :]
            attn = s.attn_low[layer, rows, :]
            grad = s.grad_out[m, block, rows, :]
            slopes, lifted = [], []
            for half in range(2):
                lanes = pl.ds(pl.multiple_of(step * LANES + half * 128, 128), 128)
                part = slice(half * 128, (half + 1) * 128)
                z = rows_of[block][p, rows, lanes] + wanted
                t = jnp.tanh(z)
                w = t + jnp.asarray(1.5, BF16)
                logit_grad = s.scores[block, step, h : h + 1, part].astype(BF16)
                share = s.shares[p, block, step, h : h + 1, part].astype(BF16)
                lifted.append(z * w * logit_grad)
                slope = (w + z * (jnp.asarray(1.0, BF16) - t * t)) * logit_grad
                slopes.append(slope)
                terms[block % 2][rows, lanes] = share * grad + attn * slope
            s.message[m, block, rows, :] = s.message[m, block, rows, :] + (
                slopes[0] + slopes[1]
            ).astype(F32)
            s.grad_vecs[layer, 0, rows, :] = s.grad_vecs[layer, 0, rows, :] + (
                lifted[0] + lifted[1]
            ).astype(F32)

    def over_steps(work):
        def body(step, carry):
            work(step)
            return carry

        lax.fori_loop(0, STEPS, body, 0)

    def big_back(p, layer, m, progress):
        spread(p, 0, True)
        over_steps(lambda step: share_grads(p, m, 0, step))
        logit_grads(p, [0])
        s.message[m] = jnp.zeros((BLOCKS, WIDTH, 128), F32)
        progress()
        over_steps(lambda step: make_terms(p, layer, m, 0, step))
        s.table[p] = nt(s.hot_big[m if kept > 1 else 0], terms[0][...]).astype(BF16)
        start(reduce_core(p))

    def scatter_small(m, b):
        here = pl.ds(b * BIG, 256)
        hot = s.hot_small[m if kept > 1 else 0, b]
        s.grad_ext[here] = s.grad_ext[here] + nt(hot, terms[(b + 1) % 2][...])

    def smalls_back(p, layer, m, progress):
        for b in range(SMALLS):
            spread(p, b + 1, True)
        for b in range(SMALLS):
            over_steps(lambda step: share_grads(p, m, b + 1, step))
        logit_grads(p, [1, 2, 3])
        s.grad_ext[...] = jnp.zeros_like(s.grad_ext)
        progress()
        over_steps(lambda step: make_terms(p, layer, m, 1, step))
        for b in range(1, SMALLS):
            scatter_small(m, b - 1)
            for step in range(STEPS):
                make_terms(p, layer, m, b + 1, step)
        scatter_small(m, SMALLS - 1)
        s.send_rim[p, 0] = s.grad_ext[pl.ds(0, RIM)].astype(BF16)
        s.send_rim[p, 1] = s.grad_ext[pl.ds(RIM + SMALL, RIM)].astype(BF16)
        start(reduce_rims(p))
        s.grad_small[m] = s.grad_ext[pl.ds(RIM, SMALL)]
        attn = s.vecs[layer, 0]
        for t in range(2):
            lanes = slice(t * 128, (t + 1) * 128)
            total = join_halves(s.message[m, 2 * t], s.message[m, 2 * t + 1])
            s.grad_targets_t[p, :, lanes] = (attn * total).astype(BF16)

    def finalise(p, layer, m):
        unit = reduced_unit(p)
        finish(reduce_rims(p))
        low = s.grad_small[m, pl.ds(0, RIM)] + s.land_rim[p, 0].astype(F32)
        high = s.grad_small[m, pl.ds(RIM, RIM)] + s.land_rim[p, 1].astype(F32)
        rows = jnp.concatenate([unit, low, high], axis=0)
        s.grad_sources_t[p] = jnp.transpose(rows.astype(BF16))
        s.grad_act[m] = (
            nn(s.weights[layer, pl.ds(0, WIDTH)], s.grad_sources_t[p])
            + nn(s.weights[layer, pl.ds(WIDTH, WIDTH)], s.grad_targets_t[p])
            + nn(s.weights[layer, pl.ds(2 * WIDTH, WIDTH)], s.grad_out_t[p])
        )

    def weight_grads(layer):
        for k, grads in enumerate((s.grad_sources_t, s.grad_targets_t, s.grad_out_t)):
            total = nt(s.hidden_t[2 * layer], grads[2 * layer]) + nt(
                s.hidden_t[2 * layer + 1], grads[2 * layer + 1]
            )
            if shared_weights:
                s.grad_weights[pl.ds(k * WIDTH, WIDTH)] = total
            else:
                s.weight_sums[layer, pl.ds(k * WIDTH, WIDTH)] = total
        vector_rows = jnp.zeros((8, WIDTH), F32)
        for k in range(4):
            chosen = jnp.where(
                lax.broadcasted_iota(jnp.int32, (8, 128), 0) == k, 2.0 if k == 0 else 1.0, 0.0
            ).astype(F32)
            vector_rows = vector_rows + nt(
                chosen, s.grad_vecs[layer, k], precision=lax.Precision.HIGHEST
            )
        if not shared_weights:
            s.vector_sums[layer] = vector_rows
            return
        for chunk, at in chunks():
            s.table[4 + layer, pl.ds(at, PIECE)] = jnp.concatenate(
                [s.grad_weights[pl.ds(chunk * CHUNK, CHUNK)], vector_rows], axis=0
            ).astype(BF16)
        start(reduce_core(4 + layer))

    def weights_on(layer):
        add_core(4 + layer)
        start(reduce_pieces(layer))

    def weights_done(layer):
        finish(reduce_pieces(layer))
        total = s.table[4 + layer, piece_rows(own_row, own_f)].astype(F32)
        for k in range(2 * len(far) + 1):
            total = total + s.land_piece[layer, k].astype(F32)
        s.weight_sums[layer : layer + 1, :] = jnp.concatenate(
            [total[i : i + 1] for i in range(CHUNK)], axis=1
        )
        own = jnp.where(own_row_of_eight(), total[CHUNK:], 0.0)
        own = jnp.sum(own, axis=0, keepdims=True)
        own = nt(
            jnp.broadcast_to(own, (8, WIDTH)), vector_place(), precision=lax.Precision.HIGHEST
        )
        s.vector_sums[layer : layer + 1, :] = own[:1]

    def backward(i, carry):
        layer = 1 - i
        first, second = 2 * layer, 2 * layer + 1

        def big_body(m, inner):
            if kept == 1:
                mark_big(m)

            @pl.when(i == 1)
            def _():
                finalise(2 + m, 1, m)

            @pl.when(jnp.logical_and(i == 1, m == 1))
            def _():
                weight_grads(1)

            def progress():
                @pl.when(m == 1)
                def _():
                    reduce_on(first)

            through_norm(first + m, layer, m)
            big_back(first + m, layer, m, progress)
            return inner

        lax.fori_loop(0, MICRO, big_body, 0)

        def small_body(m, inner):
            if kept == 1:
                mark_small(m)

            def progress():
                @pl.when(m == 0)
                def _():
                    reduce_on(second)

                if shared_weights:

                    @pl.when(jnp.logical_and(i == 1, m == 1))
                    def _():
                        weights_on(1)

            smalls_back(first + m, layer, m, progress)
            return inner

        lax.fori_loop(0, MICRO, small_body, 0)
        return carry

    barrier = pltpu.get_barrier_semaphore()
    partners = [dict(blk=peer) for peer, _ in far]
    if shared_weights:
        partners = [dict(blk=peer, fsdp=f) for peer, f, _ in all_far()]
    partners += [dict(blk=d) for d in (sibling, before, after)]
    for partner in partners:
        pl.semaphore_signal(barrier, inc=1, device_id=partner, device_id_type=MESH)
    if shared_weights:
        for layer in range(LAYERS):
            own_piece(layer)
    pl.semaphore_wait(barrier, len(partners))

    if shared_weights:
        start(gather_pieces(0))
    prepare(0)
    prepare(1)
    s.scores[...] = jnp.zeros_like(s.scores)
    s.grad_vecs[...] = jnp.zeros_like(s.grad_vecs)
    if kept > 1:
        mark_small(0)
        mark_small(1)
        mark_big(0)
        mark_big(1)
    if shared_weights:
        finish(gather_pieces(0))
        start(gather_core(4))
        start(gather_pieces(1))
        finish(gather_core(4))
    load_layer(0)
    project(0, 0, 0, s.features[0])
    project(1, 0, 1, s.features[1])
    if shared_weights:
        finish(gather_pieces(1))
        start(gather_core(5))
        finish(gather_core(5))
    load_layer(1)
    lax.fori_loop(0, LAYERS, forward, 0)
    lax.fori_loop(0, LAYERS, backward, 0)
    finalise(0, 0, 0)
    s.input_gradient[0] = jnp.transpose(s.grad_act[0])
    finalise(1, 0, 1)
    weight_grads(0)
    s.input_gradient[1] = jnp.transpose(s.grad_act[1])
    if shared_weights:
        weights_on(0)
        weights_done(1)
        weights_done(0)


def per_device(
    depth, fsdp_count, features, neighbours, slot_mask, projections, vectors, out_cotangent
):
    layers, weight_chunk = projections.shape
    shared_weights = fsdp_count == 2 and weight_chunk == CHUNK * WIDTH and depth == 4
    inputs = dict(
        features=features[:, 0],
        neighbours=jnp.swapaxes(neighbours[:, 0], 1, 2),
        slot_mask=jnp.swapaxes(slot_mask[:, 0], 1, 2),
        out_cotangent=out_cotangent[:, 0],
    )
    if shared_weights:
        inputs["projections"] = projections
        inputs["vectors"] = vectors
        weight_shape, vector_shape = projections.shape, vectors.shape
    else:
        axes = ("blk", "fsdp")
        gathered = lax.all_gather(projections, axes, axis=1, tiled=True)
        inputs["weights"] = gathered.reshape(layers, 3 * WIDTH, WIDTH)
        gathered = lax.all_gather(vectors, axes, axis=1, tiled=True)
        inputs["all_vectors"] = jnp.pad(
            gathered.reshape(layers, 4, WIDTH), ((0, 0), (0, 4), (0, 0))
        )
        weight_shape, vector_shape = (layers, 3 * WIDTH, WIDTH), (layers, 8, WIDTH)
    outputs = dict(
        layer_output=jax.ShapeDtypeStruct((MICRO, NODES, WIDTH), BF16),
        input_gradient=jax.ShapeDtypeStruct((MICRO, NODES, WIDTH), F32),
        weight_sums=jax.ShapeDtypeStruct(weight_shape, F32),
        vector_sums=jax.ShapeDtypeStruct(vector_shape, F32),
    )
    scratch = scratch_plan(depth, shared_weights)
    in_vmem = pl.BlockSpec(memory_space=pltpu.VMEM)
    layer_output, input_gradient, weight_sums, vector_sums = pl.pallas_call(
        functools.partial(
            step_kernel, depth, shared_weights, [*inputs, *outputs, *scratch]
        ),
        out_shape=list(outputs.values()),
        in_specs=[in_vmem] * len(inputs),
        out_specs=[in_vmem] * len(outputs),
        scratch_shapes=list(scratch.values()),
        compiler_params=pltpu.CompilerParams(
            collective_id=0, has_side_effects=True, vmem_limit_bytes=63 * 1024 * 1024
        ),
    )(*inputs.values())
    if not shared_weights:
        axes = ("blk", "fsdp")
        weight_sums = lax.psum_scatter(
            weight_sums.reshape(layers, -1), axes, scatter_dimension=1, tiled=True
        )
        vector_sums = lax.psum_scatter(
            vector_sums[:, :4].reshape(layers, -1), axes, scatter_dimension=1, tiled=True
        )
    return layer_output[:, None], input_gradient[:, None], weight_sums, vector_sums


def solution(mesh):
    return jax.shard_map(
        functools.partial(per_device, mesh.shape["blk"] // 4, mesh.shape["fsdp"]),
        mesh=mesh,
        in_specs=(
            P(None, "fsdp", "blk", None),
            P(None, "fsdp", "blk", None),
            P(None, "fsdp", "blk", None),
            P(None, ("blk", "fsdp")),
            P(None, ("blk", "fsdp")),
            P(None, "fsdp", "blk", None),
        ),
        out_specs=(
            P(None, "fsdp", "blk", None),
            P(None, "fsdp", "blk", None),
            P(None, ("blk", "fsdp")),
            P(None, ("blk", "fsdp")),
        ),
        check_vma=False,
    )
```

time: 169 us -> 129 us (0.76)
  Pallas kernels: 160 us -> 124 us
  local copies, waits for them, and re-layouts: 7.93 us -> 3.75 us
    pallas_call x1, Pallas kernels: 160 us -> 124 us  [per_device(): pl.pallas_call(functools.partial(step_kernel, depth, shared_weights, [*in...]
    unnamed x18 -> x10, local copies, waits for them, and re-layouts: 7.2 us -> 3.75 us
where the time goes in v2:
time: 129 us
  Pallas kernels  124 us (96%)
  local copies, waits for them, and re-layouts  3.75 us (3%)
    pallas_call x1, Pallas kernels, per_device(): pl.pallas_call(functools.partial(step_kernel, depth, shared_weights, [*in...  124 us
    unnamed x10, local copies, waits for them, and re-layouts  3.75 us

profile of v2, /device:TPU:0, one launch (start us, length us, event | category | flops | bytes accessed | tf_op | source)
XLA Modules:
  0.0 128.6 jit_solution(6337793427828318877)
XLA Ops:
  0.6 124.2 %shard_map.93 = (bf16[2,256,256]{2,1,0:T(8,128)(2,1)}, f32[2,256,256]{2,1,0:T(8,128)}, f32[2,6144]{1,0:T(2,128)}, f32[2,32]{1,0:T(2,128)}) custom-call(bf16[2,256,256]{2,1,0:T(8,128)(2,1)} %bitcast.15, s32[2,32,256]{2,1,0:T(8,128)} %bitcast.18, s32[2,32,256]{2,1,0:T(8,128)} %bitcast.19, bf16[2,256,256]{2,1,0:T(8,128)(2,1)} %bitcast.16, ...), custom_call_target="tpu_custom_call" | custom-call | tf_op jit(solution)/shard_map/pallas_call | solution.py:889
  124.8 0.0 copy-start
  124.8 1.7 %copy.16 = bf16[2,1,256,256]{3,2,1,0:T(8,128)(2,1)} copy(bf16[2,1,256,256]{3,2,1,0:T(8,128)(2,1)} %bitcast.17) | data formatting | bytes 524288
  126.5 0.0 copy-done
  126.5 0.0 copy-start.1
  126.5 0.8 copy.17
  127.3 0.0 copy-done.1
  127.3 0.0 copy-start.2
  127.3 0.6 copy.18
  128.0 0.0 copy-done.2
  128.0 0.6 copy.19
Async XLA Ops:
  124.8 1.7 %copy-start = (f32[2,256,256]{2,1,0:T(8,128)S(1)}, f32[2,256,256]{2,1,0:T(8,128)}, u32[]{:S(2)}) copy-start(f32[2,256,256]{2,1,0:T(8,128)} %get-tuple-element.9) | copy-start | bytes 1572868
  126.5 0.8 copy-start.1
  127.3 0.7 copy-start.2

commit v3 on v2

--- a/solution.py
+++ b/solution.py
@@ -81,26 +81,27 @@
         turned_big=vm((WIDTH, big_total), BF16),
         turned_small=vm((SMALLS, WIDTH, 256), BF16),
         hidden_t=vm((4, WIDTH, NODES), BF16),
-        weights_t=vm((LAYERS, 2 * WIDTH, WIDTH), BF16),
+        weights_t=vm((LAYERS, 3 * WIDTH, WIDTH), BF16),
         vecs=vm((LAYERS, 4, WIDTH, 128), F32),
-        attn_low=vm((LAYERS, WIDTH, 128), BF16),
         targets=vm((4, WIDTH, NODES), F32),
         residue=vm((MICRO, WIDTH, NODES), F32),
         doubled=vm((BLOCKS, WIDTH, 128), F32),
-        doubled_low=vm((BLOCKS, WIDTH, 128), BF16),
         scores=vm((BLOCKS, STEPS, 8, LANES), F32),
+        share_grad=vm((MICRO, BLOCKS, STEPS, 8, LANES), F32),
         message=vm((MICRO, BLOCKS, WIDTH, 128), F32),
         normed=vm((4, WIDTH, NODES), F32),
         inverse=vm((4, 8, NODES), F32),
         act=vm((WIDTH, NODES), BF16),
         grad_act=vm((MICRO, WIDTH, NODES), F32),
-        grad_out=vm((MICRO, BLOCKS, WIDTH, 128), BF16),
+        grad_out=vm((MICRO, BLOCKS, WIDTH, 128), F32),
         grad_out_t=vm((4, WIDTH, NODES), BF16),
         grad_targets_t=vm((4, WIDTH, NODES), BF16),
         grad_sources_t=vm((4, WIDTH, NODES), BF16),
-        terms_0=vm((WIDTH, PAIRS), BF16),
-        terms_1=vm((WIDTH, PAIRS), BF16),
+        terms_0=vm((WIDTH, 2 * LANES), BF16),
+        terms_1=vm((WIDTH, 2 * LANES), BF16),
+        part_sum=vm((big_total, WIDTH), F32),
         grad_ext=vm((EXT, WIDTH), F32),
+        head_weights=vm((WIDTH, WIDTH), F32),
         grad_small=vm((MICRO, SMALL, WIDTH), F32),
         grad_vecs=vm((LAYERS, 4, WIDTH, 128), F32),
         land_core=vm((tables, big_total // 2, WIDTH), BF16),
@@ -166,8 +167,10 @@
     def half_rows(c):
         return pl.ds(unit_row(0, 0, c), 2 * depth * UNIT)
 
-    def piece_rows(row, f):
-        return pl.ds(pl.multiple_of(row + f * PIECE, PIECE), PIECE)
+    def piece_row(z, x, c, f):
+        return pl.multiple_of((((c * 2 + x) * 2 + f) * depth + z) * PIECE, PIECE)
+
+    own_piece_row = piece_row(along_z, along_x, core, own_f)
 
     def gather_far(p):
         unit = s.table.at[p, pl.ds(own_row, UNIT)]
@@ -178,17 +181,32 @@
 
     def all_far():
         found = []
-        for peer, row in far:
-            for f in (1 - own_f, own_f):
-                found.append((peer, f, piece_rows(row, f)))
-        found.append((me, 1 - own_f, piece_rows(own_row, 1 - own_f)))
+        for dz in sorted(range(depth), reverse=True):
+            for dx in (1, 0):
+                for f in (1 - own_f, own_f):
+                    if dz or dx or f is not own_f:
+                        z, x = lax.rem(along_z + dz, depth), lax.rem(along_x + dx, 2)
+                        found.append((z * 4 + x * 2 + core, f, piece_row(z, x, core, f)))
         return found
 
-    def gather_pieces(layer):
-        piece = s.table.at[4 + layer, piece_rows(own_row, own_f)]
+    def gather_pieces_z(layer):
+        piece = s.table.at[4 + layer, pl.ds(own_piece_row, PIECE)]
+        peers = [
+            lax.rem(along_z + dz, depth) * 4 + along_x * 2 + core for dz in range(1, depth)
+        ]
         return [
-            remote(piece, piece, gather_sems, (4 + layer, k), blk=peer, fsdp=f)
-            for k, (peer, f, _) in enumerate(all_far())
+            remote(piece, piece, gather_sems, (4 + layer, k), blk=peer)
+            for k, peer in enumerate(reversed(peers))
+        ]
+
+    def gather_pieces_xy(layer):
+        column = piece_row(0, along_x, core, own_f)
+        piece = s.table.at[4 + layer, pl.ds(column, depth * PIECE)]
+        other = along_z * 4 + (1 - along_x) * 2 + core
+        peers = [(other, 1 - own_f), (other, own_f), (me, 1 - own_f)]
+        return [
+            remote(piece, piece, gather_sems, (4 + layer, 8 + k), blk=peer, fsdp=f)
+            for k, (peer, f) in enumerate(peers)
         ]
 
     def gather_core(q):
@@ -212,10 +230,13 @@
         )
         return [low, high]
 
+    def part_of(q):
+        return q if isinstance(q, int) and q >= 4 else 2 + lax.rem(q, 2)
+
     def reduce_core(q):
         return [
             remote(
-                s.table.at[q, half_rows(1 - core)],
+                s.table.at[part_of(q), half_rows(1 - core)],
                 s.land_core.at[q],
                 reduce_sems,
                 (q, core_slot),
@@ -226,7 +247,7 @@
     def reduce_far(p):
         return [
             remote(
-                s.table.at[p, pl.ds(row, UNIT)],
+                s.table.at[part_of(p), pl.ds(row, UNIT)],
                 s.land.at[p, k],
                 reduce_sems,
                 (p, k),
@@ -238,14 +259,14 @@
     def reduce_pieces(layer):
         return [
             remote(
-                s.table.at[4 + layer, rows],
+                s.table.at[4 + layer, pl.ds(row, PIECE)],
                 s.land_piece.at[layer, k],
                 reduce_sems,
                 (4 + layer, k),
                 blk=peer,
                 fsdp=f,
             )
-            for k, (peer, f, rows) in enumerate(all_far())
+            for k, (peer, f, row) in enumerate(all_far())
         ]
 
     def reduce_rims(p):
@@ -268,12 +289,13 @@
     def add_core(q):
         finish(reduce_core(q))
         first = unit_row(0, 0, core)
+        at = part_of(q)
 
         def body(i, carry):
             here = pl.ds(pl.multiple_of(first + i * UNIT, UNIT), UNIT)
             there = pl.ds(pl.multiple_of(i * UNIT, UNIT), UNIT)
-            s.table[q, here] = (
-                s.table[q, here].astype(F32) + s.land_core[q, there].astype(F32)
+            s.table[at, here] = (
+                s.table[at, here].astype(F32) + s.land_core[q, there].astype(F32)
             ).astype(BF16)
             return carry
 
@@ -285,7 +307,7 @@
 
     def reduced_unit(p):
         finish(reduce_far(p))
-        total = s.table[p, pl.ds(own_row, UNIT)].astype(F32)
+        total = s.table[part_of(p), pl.ds(own_row, UNIT)].astype(F32)
         for k in range(len(far)):
             total = total + s.land[p, k].astype(F32)
         return total
@@ -363,7 +385,7 @@
         own = s.vectors[...][layer : layer + 1].astype(F32)
         own = nn(jnp.broadcast_to(own, (8, 32)).astype(BF16), vector_place().astype(BF16))
         rows.append(jnp.where(own_row_of_eight(), own, 0.0))
-        s.table[4 + layer, piece_rows(own_row, own_f)] = jnp.concatenate(
+        s.table[4 + layer, pl.ds(own_piece_row, PIECE)] = jnp.concatenate(
             rows, axis=0
         ).astype(BF16)
 
@@ -374,7 +396,7 @@
                     for y in range(2):
                         yield (
                             ((z * 2 + x) * 2 + c) * 2 + y,
-                            (((c * 2 + x) * depth + z) * 2 + y) * PIECE,
+                            (((c * 2 + x) * 2 + y) * depth + z) * PIECE,
                         )
 
     def load_layer(layer):
@@ -391,49 +413,46 @@
                 rows = rows + pieces[i][CHUNK:]
         else:
             rows = s.all_vectors[layer].astype(F32)
-        for k in range(2):
-            s.weights_t[layer, pl.ds(k * WIDTH, WIDTH)] = jnp.transpose(
-                s.weights[layer, pl.ds((k + 1) * WIDTH, WIDTH)]
-            )
+        for k in range(3):
+            rows_k = pl.ds(k * WIDTH, WIDTH)
+            s.weights_t[layer, rows_k] = jnp.transpose(s.weights[layer, rows_k])
         which = lax.broadcasted_iota(jnp.int32, (8, 512), 0)
         lane = lax.shift_right_logical(lax.broadcasted_iota(jnp.int32, (8, 512), 1), 7)
         chosen = jnp.where(which == lane, 1.0, 0.0).astype(BF16)
         wide = tn(rows.astype(BF16), chosen)
         for k in range(4):
             s.vecs[layer, k] = wide[:, k * 128 : (k + 1) * 128]
-        s.attn_low[layer] = wide[:, :128].astype(BF16)
-
-    def project(p, layer, m, hidden):
-        sources = (0.5 * nn(hidden, s.weights[layer, pl.ds(0, WIDTH)])).astype(BF16)
-        s.table[p, pl.ds(own_row, UNIT)] = sources[:BIG]
-        s.ext[p, pl.ds(RIM, SMALL)] = sources[BIG:]
-        start(gather_rims(p))
-        start(gather_far(p))
-        s.targets[p] = 0.5 * nt(s.weights_t[layer, pl.ds(0, WIDTH)], hidden)
+
+    def share(p, hidden):
+        s.table[p, pl.ds(own_row, UNIT)] = hidden[:BIG]
+        s.ext[p, pl.ds(RIM, SMALL)] = hidden[BIG:]
+
+    def aim(p, layer, m, hidden):
+        s.targets[p] = 0.5 * nt(s.weights_t[layer, pl.ds(WIDTH, WIDTH)], hidden)
         bias = s.vecs[layer, 1]
-        s.residue[m] = nt(s.weights_t[layer, pl.ds(WIDTH, WIDTH)], hidden) + jnp.concatenate(
+        s.residue[m] = nt(s.weights_t[layer, pl.ds(2 * WIDTH, WIDTH)], hidden) + jnp.concatenate(
             [bias, bias], axis=1
         )
 
-    def spread(p, block, low):
+    def spread(p, block):
         wide = s.targets[p, :, pl.ds((block // 2) * 128, 128)]
         odd = block % 2 == 1
         tile = jnp.where(upper_lanes() == odd, wide, pltpu.roll(wide, 64, 1))
-        if low:
-            s.doubled_low[block] = tile.astype(BF16)
-        else:
-            s.doubled[block] = tile
-
-    def score(p, layer, block, step):
+        s.doubled[block] = tile
+
+    def score(p, layer, block, pair, turned, hot):
+        lanes = pl.ds(pair * 2 * LANES, 2 * LANES)
+        got = nn(turned[...], hot[:, lanes])
+        rows_of[block][p, :, lanes] = got.astype(BF16)
         for h in range(HEADS):
             rows = slice(h * HEAD_WIDTH, (h + 1) * HEAD_WIDTH)
             wanted = s.doubled[block, rows, :]
             attn = s.vecs[layer, 0, rows, :]
-            for half in range(2):
-                lanes = pl.ds(pl.multiple_of(step * LANES + half * 128, 128), 128)
-                z = rows_of[block][p, rows, lanes].astype(F32) + wanted
+            for part in range(4):
+                z = got[rows, part * 128 : (part + 1) * 128] + wanted
                 lifted = z * (jnp.tanh(z) + 1.5)
-                s.scores[block, step, h : h + 1, half * 128 : (half + 1) * 128] = jnp.sum(
+                half = (part % 2) * 128
+                s.scores[block, 2 * pair + part // 2, h : h + 1, half : half + 128] = jnp.sum(
                     lifted * attn, axis=0, keepdims=True
                 )
 
@@ -447,81 +466,55 @@
         tile = tile + pltpu.roll(tile, 64, 1)
         return jnp.concatenate([tile, tile], axis=1)
 
-    def softmax(p, m, blocks):
-        for block in blocks:
-            used = [s.used[m, block, pl.ds(i, 1), :] for i in range(STEPS)]
-            logits = [
-                jnp.where(used[i] > 0, 0.8 * s.scores[block, i], -1e30) for i in range(STEPS)
-            ]
-            largest = halves_max(functools.reduce(jnp.maximum, logits))
-            raised = [jnp.exp(logits[i] - largest) * used[i] for i in range(STEPS)]
-            scale = 1.0 / halves_sum(functools.reduce(jnp.add, raised))
-            for i in range(STEPS):
-                share = raised[i] * scale
-                s.shares[p, block, i] = share
-
-    def pass_message(p, m, block, step):
+    def softmax(p, m, block):
+        used = [s.used[m, block, pl.ds(i, 1), :] for i in range(STEPS)]
+        logits = [
+            jnp.where(used[i] > 0, 0.8 * s.scores[block, i], -1e30) for i in range(STEPS)
+        ]
+        largest = halves_max(functools.reduce(jnp.maximum, logits))
+        raised = [jnp.exp(logits[i] - largest) * used[i] for i in range(STEPS)]
+        scale = 1.0 / halves_sum(functools.reduce(jnp.add, raised))
+        for i in range(STEPS):
+            s.shares[p, block, i] = raised[i] * scale
+
+    def pass_messages(p, m, block):
         for h in range(HEADS):
             rows = slice(h * HEAD_WIDTH, (h + 1) * HEAD_WIDTH)
-            total = s.message[m, block, rows, :]
-            for half in range(2):
-                lanes = pl.ds(pl.multiple_of(step * LANES + half * 128, 128), 128)
-                share = s.shares[p, block, step, h : h + 1, half * 128 : (half + 1) * 128]
-                share = share.astype(BF16).astype(F32)
-                total = total + share * rows_of[block][p, rows, lanes].astype(F32)
+            total = jnp.zeros((HEAD_WIDTH, 128), F32)
+            for step in range(STEPS):
+                for half in range(2):
+                    lanes = pl.ds(step * LANES + half * 128, 128)
+                    share = s.shares[p, block, step, h : h + 1, half * 128 : (half + 1) * 128]
+                    share = share.astype(BF16).astype(F32)
+                    total = total + share * rows_of[block][p, rows, lanes].astype(F32)
             s.message[m, block, rows, :] = total
 
-    def small_rows(p, m, b, part):
-        lanes = pl.ds(part * 2 * LANES, 2 * LANES)
-        hot = s.hot_small[m if kept > 1 else 0, b, :, lanes]
-        rows_of[b + 1][p, :, lanes] = nn(s.turned_small[b], hot).astype(BF16)
-
-    def big_rows(p, m, part):
-        lanes = pl.ds(part * 2 * LANES, 2 * LANES)
-        hot = s.hot_big[m if kept > 1 else 0, :, lanes]
-        rows_of[0][p, :, lanes] = nn(s.turned_big[...], hot).astype(BF16)
-
-    def smalls(p, layer, m):
+    def sources(layer, rows):
+        return (0.5 * nt(s.weights_t[layer, pl.ds(0, WIDTH)], rows)).astype(BF16)
+
+    def smalls(p, layer, m, progress):
         finish(gather_rims(p))
         for b in range(SMALLS):
-            s.turned_small[b] = jnp.transpose(s.ext[p, pl.ds(b * BIG, 256)])
-            spread(p, b + 1, False)
-        for part in range(STEPS // 2):
-            small_rows(p, m, 0, part)
+            s.turned_small[b] = sources(layer, s.ext[p, pl.ds(b * BIG, 256)])
+            spread(p, b + 1)
         for b in range(SMALLS):
-            for step in range(STEPS):
-                score(p, layer, b + 1, step)
-                if b + 1 < SMALLS and step % 2:
-                    small_rows(p, m, b + 1, step // 2)
+            if b == 1:
+                progress()
+            hot = s.hot_small.at[m if kept > 1 else 0, b]
+            for pair in range(STEPS // 2):
+                score(p, layer, b + 1, pair, s.turned_small.at[b], hot)
+            softmax(p, m, b + 1)
 
     def big(p, layer, m):
-        def turn(w, inner):
-            here = pl.ds(pl.multiple_of(w * 256, 256), 256)
-            s.turned_big[:, here] = jnp.transpose(s.table[p, here])
-            return inner
-
-        lax.fori_loop(0, big_total // 256, turn, 0)
-        spread(p, 0, False)
-        s.message[m] = jnp.zeros((BLOCKS, WIDTH, 128), F32)
-
-        for part in range(STEPS // 2):
-            big_rows(p, m, part)
-            for block in range(1, BLOCKS):
-                for step in (2 * part, 2 * part + 1):
-                    pass_message(p, m, block, step)
-
-        def body(step, carry):
-            score(p, layer, 0, step)
-            return carry
-
-        lax.fori_loop(0, STEPS, body, 0)
-        softmax(p, m, [0])
-
-        def message_body(step, carry):
-            pass_message(p, m, 0, step)
-            return carry
-
-        lax.fori_loop(0, STEPS, message_body, 0)
+        s.turned_big[...] = sources(layer, s.table[p])
+        spread(p, 0)
+        hot = s.hot_big.at[m if kept > 1 else 0]
+        for pair in range(STEPS // 2):
+            score(p, layer, 0, pair, s.turned_big, hot)
+            if pair + 1 < BLOCKS:
+                pass_messages(p, m, pair + 1)
+        softmax(p, m, 0)
+        pass_messages(p, m, 0)
 
     def normalise(p, layer, m):
         gain, shift = s.vecs[layer, 2], s.vecs[layer, 3]
@@ -542,7 +535,11 @@
         @pl.when(layer == 0)
         def _():
             s.hidden_t[m + 2] = s.act[...]
-            project(m + 2, 1, m, jnp.transpose(s.act[...]))
+            hidden = jnp.transpose(s.act[...])
+            share(m + 2, hidden)
+            start(gather_rims(m + 2))
+            start(gather_far(m + 2))
+            aim(m + 2, 1, m, hidden)
 
         @pl.when(layer == 1)
         def _():
@@ -554,14 +551,14 @@
         def small_body(m, inner):
             if kept == 1:
                 mark_small(m)
-            smalls(first + m, layer, m)
-
-            @pl.when(m == 1)
-            def _():
-                finish(gather_far(first))
-                start(gather_core(first))
-
-            softmax(first + m, m, [1, 2, 3])
+
+            def progress():
+                @pl.when(m == 1)
+                def _():
+                    finish(gather_far(first))
+                    start(gather_core(first))
+
+            smalls(first + m, layer, m, progress)
             return inner
 
         lax.fori_loop(0, MICRO, small_body, 0)
@@ -570,12 +567,25 @@
             if kept == 1:
                 mark_big(m)
             finish(gather_core(first + m))
+            if shared_weights:
+
+                @pl.when(jnp.logical_and(layer == 0, m == 0))
+                def _():
+                    finish(gather_pieces_xy(1))
+                    start(gather_core(5))
+
             big(first + m, layer, m)
 
             @pl.when(m == 0)
             def _():
                 finish(gather_far(second))
                 start(gather_core(second))
+
+            @pl.when(jnp.logical_and(layer == 0, m == 0))
+            def _():
+                if shared_weights:
+                    finish(gather_core(5))
+                load_layer(1)
 
             normalise(first + m, layer, m)
             return inner
@@ -601,9 +611,10 @@
             grad = s.inverse[p, 0:1, lanes] * (grad - first - normed * second)
             s.grad_vecs[layer, 1] = s.grad_vecs[layer, 1] + grad
             s.grad_out_t[p, :, lanes] = grad.astype(BF16)
+            grad = grad.astype(BF16).astype(F32)
             other = pltpu.roll(grad, 64, 1)
-            s.grad_out[m, 2 * t] = jnp.where(upper, other, grad).astype(BF16)
-            s.grad_out[m, 2 * t + 1] = jnp.where(upper, grad, other).astype(BF16)
+            s.grad_out[m, 2 * t] = jnp.where(upper, other, grad)
+            s.grad_out[m, 2 * t + 1] = jnp.where(upper, grad, other)
 
     def share_grads(p, m, block, step):
         for h in range(HEADS):
@@ -611,84 +622,80 @@
             grad = s.grad_out[m, block, rows, :]
             for half in range(2):
                 lanes = pl.ds(pl.multiple_of(step * LANES + half * 128, 128), 128)
-                product = rows_of[block][p, rows, lanes] * grad
-                s.scores[block, step, h : h + 1, half * 128 : (half + 1) * 128] = jnp.sum(
-                    product.astype(F32), axis=0, keepdims=True
+                product = rows_of[block][p, rows, lanes].astype(F32) * grad
+                s.share_grad[m, block, step, h : h + 1, half * 128 : (half + 1) * 128] = (
+                    jnp.sum(product, axis=0, keepdims=True)
                 )
 
-    def logit_grads(p, blocks):
-        for block in blocks:
-            shares = [s.shares[p, block, i] for i in range(STEPS)]
-            total = halves_sum(
-                functools.reduce(
-                    jnp.add, [shares[i] * s.scores[block, i] for i in range(STEPS)]
-                )
-            )
-            for i in range(STEPS):
-                s.scores[block, i] = 0.8 * shares[i] * (s.scores[block, i] - total)
-
-    def make_terms(p, layer, m, block, step):
+    def logit_grads(p, m, block):
+        shares = [s.shares[p, block, i] for i in range(STEPS)]
+        grads = [s.share_grad[m, block, i] for i in range(STEPS)]
+        total = halves_sum(functools.reduce(jnp.add, [a * b for a, b in zip(shares, grads)]))
+        for i in range(STEPS):
+            s.share_grad[m, block, i] = 0.8 * shares[i] * (grads[i] - total)
+
+    def make_terms(p, layer, m, block, pair):
         for h in range(HEADS):
             rows = slice(h * HEAD_WIDTH, (h + 1) * HEAD_WIDTH)
-            wanted = s.doubled_low[block, rows, :]
-            attn = s.attn_low[layer, rows, :]
+            wanted = s.doubled[block, rows, :]
+            attn = s.vecs[layer, 0, rows, :]
             grad = s.grad_out[m, block, rows, :]
-            slopes, lifted = [], []
-            for half in range(2):
-                lanes = pl.ds(pl.multiple_of(step * LANES + half * 128, 128), 128)
-                part = slice(half * 128, (half + 1) * 128)
-                z = rows_of[block][p, rows, lanes] + wanted
+            target_sum = s.message[m, block, rows, :]
+            attn_sum = s.grad_vecs[layer, 0, rows, :]
+            for part in range(4):
+                step, half = 2 * pair + part // 2, (part % 2) * 128
+                lanes = pl.ds(step * LANES + half, 128)
+                z = rows_of[block][p, rows, lanes].astype(F32) + wanted
                 t = jnp.tanh(z)
-                w = t + jnp.asarray(1.5, BF16)
-                logit_grad = s.scores[block, step, h : h + 1, part].astype(BF16)
-                share = s.shares[p, block, step, h : h + 1, part].astype(BF16)
-                lifted.append(z * w * logit_grad)
-                slope = (w + z * (jnp.asarray(1.0, BF16) - t * t)) * logit_grad
-                slopes.append(slope)
-                terms[block % 2][rows, lanes] = share * grad + attn * slope
-            s.message[m, block, rows, :] = s.message[m, block, rows, :] + (
-                slopes[0] + slopes[1]
-            ).astype(F32)
-            s.grad_vecs[layer, 0, rows, :] = s.grad_vecs[layer, 0, rows, :] + (
-                lifted[0] + lifted[1]
-            ).astype(F32)
-
-    def over_steps(work):
-        def body(step, carry):
-            work(step)
-            return carry
-
-        lax.fori_loop(0, STEPS, body, 0)
-
-    def big_back(p, layer, m, progress):
-        spread(p, 0, True)
-        over_steps(lambda step: share_grads(p, m, 0, step))
-        logit_grads(p, [0])
+                w = t + 1.5
+                logit_grad = s.share_grad[m, block, step, h : h + 1, half : half + 128]
+                attn_sum = attn_sum + logit_grad * (z * w)
+                slope = logit_grad * (w + z * (1.0 - t * t))
+                target_sum = target_sum + slope
+                share = s.shares[p, block, step, h : h + 1, half : half + 128]
+                share = share.astype(BF16).astype(F32)
+                terms[pair % 2][rows, part * 128 : (part + 1) * 128] = (
+                    share * grad + attn * slope
+                ).astype(BF16)
+            s.message[m, block, rows, :] = target_sum
+            s.grad_vecs[layer, 0, rows, :] = attn_sum
+
+    def all_share_grads(p, m, block):
+        for step in range(STEPS):
+            share_grads(p, m, block, step)
+        logit_grads(p, m, block)
+
+    def big_back(p, layer, m):
+        spread(p, 0)
         s.message[m] = jnp.zeros((BLOCKS, WIDTH, 128), F32)
-        progress()
-        over_steps(lambda step: make_terms(p, layer, m, 0, step))
-        s.table[p] = nt(s.hot_big[m if kept > 1 else 0], terms[0][...]).astype(BF16)
-        start(reduce_core(p))
-
-    def scatter_small(m, b):
-        here = pl.ds(b * BIG, 256)
-        hot = s.hot_small[m if kept > 1 else 0, b]
-        s.grad_ext[here] = s.grad_ext[here] + nt(hot, terms[(b + 1) % 2][...])
+        all_share_grads(p, m, 0)
+        for pair in range(STEPS // 2):
+            make_terms(p, layer, m, 0, pair)
+            lanes = pl.ds(pair * 2 * LANES, 2 * LANES)
+            added = nt(s.hot_big[m if kept > 1 else 0, :, lanes], terms[pair % 2][...])
+            if pair == 0:
+                s.part_sum[...] = added
+            elif pair + 1 < STEPS // 2:
+                s.part_sum[...] = s.part_sum[...] + added
+            else:
+                s.table[2 + m] = (s.part_sum[...] + added).astype(BF16)
 
     def smalls_back(p, layer, m, progress):
         for b in range(SMALLS):
-            spread(p, b + 1, True)
+            spread(p, b + 1)
+        s.grad_ext[...] = jnp.zeros_like(s.grad_ext)
+        all_share_grads(p, m, 1)
         for b in range(SMALLS):
-            over_steps(lambda step: share_grads(p, m, b + 1, step))
-        logit_grads(p, [1, 2, 3])
-        s.grad_ext[...] = jnp.zeros_like(s.grad_ext)
-        progress()
-        over_steps(lambda step: make_terms(p, layer, m, 1, step))
-        for b in range(1, SMALLS):
-            scatter_small(m, b - 1)
-            for step in range(STEPS):
-                make_terms(p, layer, m, b + 1, step)
-        scatter_small(m, SMALLS - 1)
+            if b == 1:
+                progress()
+            if b + 1 < SMALLS:
+                all_share_grads(p, m, b + 2)
+            here = pl.ds(b * BIG, 256)
+            for pair in range(STEPS // 2):
+                make_terms(p, layer, m, b + 1, pair)
+                lanes = pl.ds(pair * 2 * LANES, 2 * LANES)
+                hot = s.hot_small[m if kept > 1 else 0, b, :, lanes]
+                s.grad_ext[here] = s.grad_ext[here] + nt(hot, terms[pair % 2][...])
         s.send_rim[p, 0] = s.grad_ext[pl.ds(0, RIM)].astype(BF16)
         s.send_rim[p, 1] = s.grad_ext[pl.ds(RIM + SMALL, RIM)].astype(BF16)
         start(reduce_rims(p))
@@ -714,9 +721,11 @@
 
     def weight_grads(layer):
         for k, grads in enumerate((s.grad_sources_t, s.grad_targets_t, s.grad_out_t)):
-            total = nt(s.hidden_t[2 * layer], grads[2 * layer]) + nt(
-                s.hidden_t[2 * layer + 1], grads[2 * layer + 1]
-            )
+            total = nt(s.hidden_t[2 * layer], grads[2 * layer])
+            if layer == 0 and k == 0:
+                total = total + s.head_weights[...] + tn(s.ext[1], s.grad_ext[...].astype(BF16))
+            else:
+                total = total + nt(s.hidden_t[2 * layer + 1], grads[2 * layer + 1])
             if shared_weights:
                 s.grad_weights[pl.ds(k * WIDTH, WIDTH)] = total
             else:
@@ -744,7 +753,7 @@
 
     def weights_done(layer):
         finish(reduce_pieces(layer))
-        total = s.table[4 + layer, piece_rows(own_row, own_f)].astype(F32)
+        total = s.table[4 + layer, pl.ds(own_piece_row, PIECE)].astype(F32)
         for k in range(2 * len(far) + 1):
             total = total + s.land_piece[layer, k].astype(F32)
         s.weight_sums[layer : layer + 1, :] = jnp.concatenate(
@@ -761,48 +770,41 @@
         layer = 1 - i
         first, second = 2 * layer, 2 * layer + 1
 
-        def big_body(m, inner):
+        def body(m, inner):
             if kept == 1:
                 mark_big(m)
-
-            @pl.when(i == 1)
+                mark_small(m)
+
+            @pl.when(jnp.logical_and(i == 1, m == 0))
             def _():
-                finalise(2 + m, 1, m)
+                finalise(2, 1, 0)
+
+            through_norm(first + m, layer, m)
+            big_back(first + m, layer, m)
 
             @pl.when(jnp.logical_and(i == 1, m == 1))
             def _():
+                s.head_weights[...] = tn(s.table[1], s.table[3])
+
+            start(reduce_core(first + m))
+
+            @pl.when(jnp.logical_and(i == 1, m == 0))
+            def _():
+                finalise(3, 1, 1)
                 weight_grads(1)
 
             def progress():
-                @pl.when(m == 1)
-                def _():
-                    reduce_on(first)
-
-            through_norm(first + m, layer, m)
-            big_back(first + m, layer, m, progress)
-            return inner
-
-        lax.fori_loop(0, MICRO, big_body, 0)
-
-        def small_body(m, inner):
-            if kept == 1:
-                mark_small(m)
-
-            def progress():
-                @pl.when(m == 0)
-                def _():
-                    reduce_on(second)
-
+                reduce_on(first + m)
                 if shared_weights:
 
-                    @pl.when(jnp.logical_and(i == 1, m == 1))
+                    @pl.when(jnp.logical_and(i == 1, m == 0))
                     def _():
                         weights_on(1)
 
             smalls_back(first + m, layer, m, progress)
             return inner
 
-        lax.fori_loop(0, MICRO, small_body, 0)
+        lax.fori_loop(0, MICRO, body, 0)
         return carry
 
     barrier = pltpu.get_barrier_semaphore()
@@ -818,40 +820,63 @@
     pl.semaphore_wait(barrier, len(partners))
 
     if shared_weights:
-        start(gather_pieces(0))
-    prepare(0)
-    prepare(1)
+        for layer in range(LAYERS):
+            start(gather_pieces_z(layer))
+    for m in range(MICRO):
+        share(m, s.features[m])
+        start(gather_rims(m))
+    for m in range(MICRO):
+        prepare(m)
+    if not shared_weights:
+        start(gather_far(0))
+        start(gather_far(1))
     s.scores[...] = jnp.zeros_like(s.scores)
+    s.share_grad[...] = jnp.zeros_like(s.share_grad)
     s.grad_vecs[...] = jnp.zeros_like(s.grad_vecs)
     if kept > 1:
         mark_small(0)
         mark_small(1)
+    if shared_weights:
+        finish(gather_pieces_z(0))
+        start(gather_pieces_xy(0))
+        finish(gather_pieces_z(1))
+        start(gather_far(0))
+    if kept > 1:
         mark_big(0)
         mark_big(1)
     if shared_weights:
-        finish(gather_pieces(0))
+        finish(gather_pieces_xy(0))
         start(gather_core(4))
-        start(gather_pieces(1))
+        start(gather_pieces_xy(1))
+        start(gather_far(1))
         finish(gather_core(4))
     load_layer(0)
-    project(0, 0, 0, s.features[0])
-    project(1, 0, 1, s.features[1])
-    if shared_weights:
-        finish(gather_pieces(1))
-        start(gather_core(5))
-        finish(gather_core(5))
-    load_layer(1)
+    for m in range(MICRO):
+        aim(m, 0, m, s.features[m])
     lax.fori_loop(0, LAYERS, forward, 0)
     lax.fori_loop(0, LAYERS, backward, 0)
     finalise(0, 0, 0)
+    weight_grads(0)
     s.input_gradient[0] = jnp.transpose(s.grad_act[0])
+    if shared_weights:
+        weights_on(0)
     finalise(1, 0, 1)
-    weight_grads(0)
     s.input_gradient[1] = jnp.transpose(s.grad_act[1])
     if shared_weights:
-        weights_on(0)
         weights_done(1)
         weights_done(0)
+
+
+def hand_over(*refs):
+    *arrays, sems = refs
+    count = len(arrays) // 2
+    copies = [
+        pltpu.make_async_copy(arrays[k], arrays[count + k], sems.at[k]) for k in range(count)
+    ]
+    for copy in copies:
+        copy.start()
+    for copy in copies:
+        copy.wait()
 
 
 def per_device(
@@ -886,7 +911,7 @@
     )
     scratch = scratch_plan(depth, shared_weights)
     in_vmem = pl.BlockSpec(memory_space=pltpu.VMEM)
-    layer_output, input_gradient, weight_sums, vector_sums = pl.pallas_call(
+    results = pl.pallas_call(
         functools.partial(
             step_kernel, depth, shared_weights, [*inputs, *outputs, *scratch]
         ),
@@ -898,6 +923,15 @@
             collective_id=0, has_side_effects=True, vmem_limit_bytes=63 * 1024 * 1024
         ),
     )(*inputs.values())
+    if shared_weights:
+        results = pl.pallas_call(
+            hand_over,
+            out_shape=list(outputs.values()),
+            in_specs=[pl.BlockSpec(memory_space=pl.ANY)] * len(outputs),
+            out_specs=[in_vmem] * len(outputs),
+            scratch_shapes=[pltpu.SemaphoreType.DMA((len(outputs),))],
+        )(*results)
+    layer_output, input_gradient, weight_sums, vector_sums = results
     if not shared_weights:
         axes = ("blk", "fsdp")
         weight_sums = lax.psum_scatter(

time: 129 us -> 108 us (0.84)
  Pallas kernels: 124 us -> 107 us
  local copies, waits for them, and re-layouts: 3.75 us -> 0 us
    pallas_call x1, Pallas kernels: 124 us -> 105 us  [per_device(): pl.pallas_call(functools.partial(step_kernel, depth, shared_weights, [*in...]
    unnamed x10 -> x0, local copies, waits for them, and re-layouts: 3.75 us -> none
    pallas_call x0 -> x1, Pallas kernels: none -> 2.04 us  [per_device(): pl.pallas_call(hand_over, out_shape=list(outputs.values()), in_specs=[pl....]
where the time goes in v3:
time: 108 us
  Pallas kernels  107 us (99%)
    pallas_call x1, Pallas kernels, per_device(): pl.pallas_call(functools.partial(step_kernel, depth, shared_weights, [*in...  105 us

profile of v3, /device:TPU:0, one launch (start us, length us, event | category | flops | bytes accessed | tf_op | source)
XLA Modules:
  0.0 107.6 jit_solution(14648257525115772358)
XLA Ops:
  0.6 104.8 %shard_map.93 = (bf16[2,256,256]{2,1,0:T(8,128)(2,1)}, f32[2,256,256]{2,1,0:T(8,128)}, f32[2,6144]{1,0:T(2,128)}, f32[2,32]{1,0:T(2,128)}) custom-call(bf16[2,256,256]{2,1,0:T(8,128)(2,1)} %bitcast.14, s32[2,32,256]{2,1,0:T(8,128)} %bitcast.16, s32[2,32,256]{2,1,0:T(8,128)} %bitcast.17, bf16[2,256,256]{2,1,0:T(8,128)(2,1)} %bitcast.15, ...), custom_call_target="tpu_custom_call" | custom-call | tf_op jit(solution)/shard_map/pallas_call | solution.py:914
  105.4 2.0 %shard_map.94 = (bf16[2,256,256]{2,1,0:T(8,128)(2,1)}, f32[2,256,256]{2,1,0:T(8,128)}, f32[2,6144]{1,0:T(2,128)}, f32[2,32]{1,0:T(2,128)}) custom-call(bf16[2,256,256]{2,1,0:T(8,128)(2,1)} %get-tuple-element.12.refs_0_, f32[2,256,256]{2,1,0:T(8,128)} %get-tuple-element.13.refs_1_, f32[2,6144]{1,0:T(2,128)} %get-tuple-element.14.refs_2_, ...), custom_call_target="tpu_custom_call" | custom-call | tf_op jit(solution)/shard_map/pallas_call | solution.py:927

commit v4 on v3

--- a/solution.py
+++ b/solution.py
@@ -67,14 +67,21 @@
     peers = 2 * depth - 1
     vm = pltpu.VMEM
     plan = dict(
-        hot_big=vm((copies, big_total, PAIRS), BF16),
-        hot_small=vm((copies, SMALLS, 256, PAIRS), BF16),
+        features=vm((MICRO, NODES, WIDTH), BF16),
+        neighbours=vm((MICRO, SLOTS, NODES), jnp.int32),
+        slot_mask=vm((MICRO, SLOTS, NODES), jnp.int32),
+        out_cotangent=vm((MICRO, NODES, WIDTH), BF16),
+        layer_output=vm((MICRO, NODES, WIDTH), BF16),
+        input_gradient=vm((MICRO, NODES, WIDTH), F32),
+        own_sems=pltpu.SemaphoreType.DMA((7,)),
+        hot_big=vm((copies, STEPS // 2, big_total, 2 * LANES), BF16),
+        hot_small=vm((copies, SMALLS, STEPS // 2, 256, 2 * LANES), BF16),
         place=vm((MICRO, BLOCKS, STEPS, LANES), jnp.int32),
         used=vm((MICRO, BLOCKS, STEPS, LANES), F32),
-        rows_0=vm((4, WIDTH, PAIRS), BF16),
-        rows_1=vm((4, WIDTH, PAIRS), BF16),
-        rows_2=vm((4, WIDTH, PAIRS), BF16),
-        rows_3=vm((4, WIDTH, PAIRS), BF16),
+        rows_0=vm((4, 2 * STEPS, WIDTH, 128), BF16),
+        rows_1=vm((4, 2 * STEPS, WIDTH, 128), BF16),
+        rows_2=vm((4, 2 * STEPS, WIDTH, 128), BF16),
+        rows_3=vm((4, 2 * STEPS, WIDTH, 128), BF16),
         shares=vm((4, BLOCKS, STEPS, 8, LANES), F32),
         table=vm((tables, big_total, WIDTH), BF16),
         ext=vm((4, EXT, WIDTH), BF16),
@@ -278,6 +285,17 @@
         )
         return [low, high]
 
+    def bring(k, name):
+        return [
+            pltpu.make_async_copy(getattr(s, name + "_hbm"), getattr(s, name), s.own_sems.at[k])
+        ]
+
+    def hand_out(k, name, m=None):
+        kept_ref, out_ref = getattr(s, name), getattr(s, name + "_hbm")
+        if m is not None:
+            kept_ref, out_ref = kept_ref.at[m], out_ref.at[m]
+        return [pltpu.make_async_copy(kept_ref, out_ref, s.own_sems.at[k])]
+
     def start(copies):
         for copy in copies:
             copy.start()
@@ -349,9 +367,9 @@
         def tile(w, carry):
             here = pl.ds(pl.multiple_of(w * 256, 256), 256)
             for step in range(STEPS):
-                lanes = pl.ds(step * LANES, LANES)
+                lanes = pl.ds(step % 2 * LANES, LANES)
                 row = s.place[m, 0, pl.ds(step, 1), :]
-                s.hot_big[slot, here, lanes] = mark(row, w * 256)
+                s.hot_big[slot, step // 2, here, lanes] = mark(row, w * 256)
             return carry
 
         lax.fori_loop(0, big_total // 256, tile, 0)
@@ -361,9 +379,9 @@
 
         def block_body(b, carry):
             for step in range(STEPS):
-                lanes = pl.ds(step * LANES, LANES)
+                lanes = pl.ds(step % 2 * LANES, LANES)
                 row = s.place[m, b + 1, pl.ds(step, 1), :]
-                s.hot_small[slot, b, :, lanes] = mark(row, 0)
+                s.hot_small[slot, b, step // 2, :, lanes] = mark(row, 0)
             return carry
 
         lax.fori_loop(0, SMALLS, block_body, 0)
@@ -441,9 +459,10 @@
         s.doubled[block] = tile
 
     def score(p, layer, block, pair, turned, hot):
-        lanes = pl.ds(pair * 2 * LANES, 2 * LANES)
-        got = nn(turned[...], hot[:, lanes])
-        rows_of[block][p, :, lanes] = got.astype(BF16)
+        got = nn(turned[...], hot[pair])
+        low = got.astype(BF16)
+        for part in range(4):
+            rows_of[block][p, 4 * pair + part] = low[:, part * 128 : (part + 1) * 128]
         for h in range(HEADS):
             rows = slice(h * HEAD_WIDTH, (h + 1) * HEAD_WIDTH)
             wanted = s.doubled[block, rows, :]
@@ -483,10 +502,9 @@
             total = jnp.zeros((HEAD_WIDTH, 128), F32)
             for step in range(STEPS):
                 for half in range(2):
-                    lanes = pl.ds(step * LANES + half * 128, 128)
                     share = s.shares[p, block, step, h : h + 1, half * 128 : (half + 1) * 128]
                     share = share.astype(BF16).astype(F32)
-                    total = total + share * rows_of[block][p, rows, lanes].astype(F32)
+                    total = total + share * rows_of[block][p, 2 * step + half, rows].astype(F32)
             s.message[m, block, rows, :] = total
 
     def sources(layer, rows):
@@ -498,7 +516,7 @@
             s.turned_small[b] = sources(layer, s.ext[p, pl.ds(b * BIG, 256)])
             spread(p, b + 1)
         for b in range(SMALLS):
-            if b == 1:
+            if b == 2:
                 progress()
             hot = s.hot_small.at[m if kept > 1 else 0, b]
             for pair in range(STEPS // 2):
@@ -546,27 +564,17 @@
             s.layer_output[m] = jnp.transpose(s.act[...])
 
     def forward(layer, carry):
-        first, second = 2 * layer, 2 * layer + 1
-
-        def small_body(m, inner):
+        def body(m, inner):
+            p = 2 * layer + m
             if kept == 1:
                 mark_small(m)
+                mark_big(m)
 
             def progress():
-                @pl.when(m == 1)
-                def _():
-                    finish(gather_far(first))
-                    start(gather_core(first))
-
-            smalls(first + m, layer, m, progress)
-            return inner
-
-        lax.fori_loop(0, MICRO, small_body, 0)
-
-        def big_body(m, inner):
-            if kept == 1:
-                mark_big(m)
-            finish(gather_core(first + m))
+                finish(gather_far(p))
+                start(gather_core(p))
+
+            smalls(p, layer, m, progress)
             if shared_weights:
 
                 @pl.when(jnp.logical_and(layer == 0, m == 0))
@@ -574,12 +582,8 @@
                     finish(gather_pieces_xy(1))
                     start(gather_core(5))
 
-            big(first + m, layer, m)
-
-            @pl.when(m == 0)
-            def _():
-                finish(gather_far(second))
-                start(gather_core(second))
+            finish(gather_core(p))
+            big(p, layer, m)
 
             @pl.when(jnp.logical_and(layer == 0, m == 0))
             def _():
@@ -587,10 +591,10 @@
                     finish(gather_core(5))
                 load_layer(1)
 
-            normalise(first + m, layer, m)
+            normalise(p, layer, m)
             return inner
 
-        lax.fori_loop(0, MICRO, big_body, 0)
+        lax.fori_loop(0, MICRO, body, 0)
         return carry
 
     def through_norm(p, layer, m):
@@ -621,8 +625,7 @@
             rows = slice(h * HEAD_WIDTH, (h + 1) * HEAD_WIDTH)
             grad = s.grad_out[m, block, rows, :]
             for half in range(2):
-                lanes = pl.ds(pl.multiple_of(step * LANES + half * 128, 128), 128)
-                product = rows_of[block][p, rows, lanes].astype(F32) * grad
+                product = rows_of[block][p, 2 * step + half, rows].astype(F32) * grad
                 s.share_grad[m, block, step, h : h + 1, half * 128 : (half + 1) * 128] = (
                     jnp.sum(product, axis=0, keepdims=True)
                 )
@@ -644,8 +647,7 @@
             attn_sum = s.grad_vecs[layer, 0, rows, :]
             for part in range(4):
                 step, half = 2 * pair + part // 2, (part % 2) * 128
-                lanes = pl.ds(step * LANES + half, 128)
-                z = rows_of[block][p, rows, lanes].astype(F32) + wanted
+                z = rows_of[block][p, 4 * pair + part, rows].astype(F32) + wanted
                 t = jnp.tanh(z)
                 w = t + 1.5
                 logit_grad = s.share_grad[m, block, step, h : h + 1, half : half + 128]
@@ -671,8 +673,7 @@
         all_share_grads(p, m, 0)
         for pair in range(STEPS // 2):
             make_terms(p, layer, m, 0, pair)
-            lanes = pl.ds(pair * 2 * LANES, 2 * LANES)
-            added = nt(s.hot_big[m if kept > 1 else 0, :, lanes], terms[pair % 2][...])
+            added = nt(s.hot_big[m if kept > 1 else 0, pair], terms[pair % 2][...])
             if pair == 0:
                 s.part_sum[...] = added
             elif pair + 1 < STEPS // 2:
@@ -693,8 +694,7 @@
             here = pl.ds(b * BIG, 256)
             for pair in range(STEPS // 2):
                 make_terms(p, layer, m, b + 1, pair)
-                lanes = pl.ds(pair * 2 * LANES, 2 * LANES)
-                hot = s.hot_small[m if kept > 1 else 0, b, :, lanes]
+                hot = s.hot_small[m if kept > 1 else 0, b, pair]
                 s.grad_ext[here] = s.grad_ext[here] + nt(hot, terms[pair % 2][...])
         s.send_rim[p, 0] = s.grad_ext[pl.ds(0, RIM)].astype(BF16)
         s.send_rim[p, 1] = s.grad_ext[pl.ds(RIM + SMALL, RIM)].astype(BF16)
@@ -706,18 +706,24 @@
             total = join_halves(s.message[m, 2 * t], s.message[m, 2 * t + 1])
             s.grad_targets_t[p, :, lanes] = (attn * total).astype(BF16)
 
-    def finalise(p, layer, m):
+    def finalise_sources(p, m):
         unit = reduced_unit(p)
         finish(reduce_rims(p))
         low = s.grad_small[m, pl.ds(0, RIM)] + s.land_rim[p, 0].astype(F32)
         high = s.grad_small[m, pl.ds(RIM, RIM)] + s.land_rim[p, 1].astype(F32)
         rows = jnp.concatenate([unit, low, high], axis=0)
         s.grad_sources_t[p] = jnp.transpose(rows.astype(BF16))
+
+    def finalise_hidden(p, layer, m):
         s.grad_act[m] = (
             nn(s.weights[layer, pl.ds(0, WIDTH)], s.grad_sources_t[p])
             + nn(s.weights[layer, pl.ds(WIDTH, WIDTH)], s.grad_targets_t[p])
             + nn(s.weights[layer, pl.ds(2 * WIDTH, WIDTH)], s.grad_out_t[p])
         )
+
+    def finalise(p, layer, m):
+        finalise_sources(p, m)
+        finalise_hidden(p, layer, m)
 
     def weight_grads(layer):
         for k, grads in enumerate((s.grad_sources_t, s.grad_targets_t, s.grad_out_t)):
@@ -814,6 +820,9 @@
     partners += [dict(blk=d) for d in (sibling, before, after)]
     for partner in partners:
         pl.semaphore_signal(barrier, inc=1, device_id=partner, device_id_type=MESH)
+    brought = ("features", "neighbours", "slot_mask", "out_cotangent")
+    for k, name in enumerate(brought):
+        start(bring(k, name))
     if shared_weights:
         for layer in range(LAYERS):
             own_piece(layer)
@@ -822,9 +831,12 @@
     if shared_weights:
         for layer in range(LAYERS):
             start(gather_pieces_z(layer))
+    finish(bring(0, "features"))
     for m in range(MICRO):
         share(m, s.features[m])
         start(gather_rims(m))
+    for k in (1, 2, 3):
+        finish(bring(k, brought[k]))
     for m in range(MICRO):
         prepare(m)
     if not shared_weights:
@@ -854,17 +866,24 @@
     for m in range(MICRO):
         aim(m, 0, m, s.features[m])
     lax.fori_loop(0, LAYERS, forward, 0)
+    start(hand_out(4, "layer_output"))
     lax.fori_loop(0, LAYERS, backward, 0)
-    finalise(0, 0, 0)
+    finalise_sources(0, 0)
     weight_grads(0)
-    s.input_gradient[0] = jnp.transpose(s.grad_act[0])
+    finalise_hidden(0, 0, 0)
     if shared_weights:
         weights_on(0)
+    s.input_gradient[0] = jnp.transpose(s.grad_act[0])
+    start(hand_out(5, "input_gradient", 0))
     finalise(1, 0, 1)
     s.input_gradient[1] = jnp.transpose(s.grad_act[1])
+    start(hand_out(6, "input_gradient", 1))
     if shared_weights:
         weights_done(1)
         weights_done(0)
+    finish(hand_out(4, "layer_output"))
+    for m in range(MICRO):
+        finish(hand_out(5 + m, "input_gradient", m))
 
 
 def hand_over(*refs):
@@ -885,10 +904,10 @@
     layers, weight_chunk = projections.shape
     shared_weights = fsdp_count == 2 and weight_chunk == CHUNK * WIDTH and depth == 4
     inputs = dict(
-        features=features[:, 0],
-        neighbours=jnp.swapaxes(neighbours[:, 0], 1, 2),
-        slot_mask=jnp.swapaxes(slot_mask[:, 0], 1, 2),
-        out_cotangent=out_cotangent[:, 0],
+        features_hbm=features[:, 0],
+        neighbours_hbm=jnp.swapaxes(neighbours[:, 0], 1, 2),
+        slot_mask_hbm=jnp.swapaxes(slot_mask[:, 0], 1, 2),
+        out_cotangent_hbm=out_cotangent[:, 0],
     )
     if shared_weights:
         inputs["projections"] = projections
@@ -904,20 +923,21 @@
         )
         weight_shape, vector_shape = (layers, 3 * WIDTH, WIDTH), (layers, 8, WIDTH)
     outputs = dict(
-        layer_output=jax.ShapeDtypeStruct((MICRO, NODES, WIDTH), BF16),
-        input_gradient=jax.ShapeDtypeStruct((MICRO, NODES, WIDTH), F32),
+        layer_output_hbm=jax.ShapeDtypeStruct((MICRO, NODES, WIDTH), BF16),
+        input_gradient_hbm=jax.ShapeDtypeStruct((MICRO, NODES, WIDTH), F32),
         weight_sums=jax.ShapeDtypeStruct(weight_shape, F32),
         vector_sums=jax.ShapeDtypeStruct(vector_shape, F32),
     )
     scratch = scratch_plan(depth, shared_weights)
     in_vmem = pl.BlockSpec(memory_space=pltpu.VMEM)
+    in_hbm = pl.BlockSpec(memory_space=pl.ANY)
     results = pl.pallas_call(
         functools.partial(
             step_kernel, depth, shared_weights, [*inputs, *outputs, *scratch]
         ),
         out_shape=list(outputs.values()),
-        in_specs=[in_vmem] * len(inputs),
-        out_specs=[in_vmem] * len(outputs),
+        in_specs=[in_hbm if name.endswith("_hbm") else in_vmem for name in inputs],
+        out_specs=[in_hbm if name.endswith("_hbm") else in_vmem for name in outputs],
         scratch_shapes=list(scratch.values()),
         compiler_params=pltpu.CompilerParams(
             collective_id=0, has_side_effects=True, vmem_limit_bytes=63 * 1024 * 1024
@@ -927,7 +947,7 @@
         results = pl.pallas_call(
             hand_over,
             out_shape=list(outputs.values()),
-            in_specs=[pl.BlockSpec(memory_space=pl.ANY)] * len(outputs),
+            in_specs=[in_hbm] * len(outputs),
             out_specs=[in_vmem] * len(outputs),
             scratch_shapes=[pltpu.SemaphoreType.DMA((len(outputs),))],
         )(*results)

time: 108 us -> 103 us (0.954)
  Pallas kernels: 107 us -> 102 us
    pallas_call x1, Pallas kernels: 105 us -> 99.8 us  [per_device(): pl.pallas_call(functools.partial(step_kernel, depth, shared_weights, [*in...]
where the time goes in v4:
time: 103 us
  Pallas kernels  102 us (99%)
    pallas_call x1, Pallas kernels, per_device(): pl.pallas_call(functools.partial(step_kernel, depth, shared_weights, [*in...  99.8 us

profile of v4, /device:TPU:0, one launch (start us, length us, event | category | flops | bytes accessed | tf_op | source)
XLA Modules:
  0.0 102.7 jit_solution(10301800871664656377)
XLA Ops:
  0.6 99.8 %shard_map.93 = (bf16[2,256,256]{2,1,0:T(8,128)(2,1)}, f32[2,256,256]{2,1,0:T(8,128)}, f32[2,6144]{1,0:T(2,128)}, f32[2,32]{1,0:T(2,128)}) custom-call(bf16[2,256,256]{2,1,0:T(8,128)(2,1)} %bitcast.14, s32[2,32,256]{2,1,0:T(8,128)} %bitcast.16, s32[2,32,256]{2,1,0:T(8,128)} %bitcast.17, bf16[2,256,256]{2,1,0:T(8,128)(2,1)} %bitcast.15, ...), custom_call_target="tpu_custom_call" | custom-call | tf_op jit(solution)/shard_map/pallas_call | solution.py:934
  100.5 2.0 %shard_map.94 = (bf16[2,256,256]{2,1,0:T(8,128)(2,1)}, f32[2,256,256]{2,1,0:T(8,128)}, f32[2,6144]{1,0:T(2,128)}, f32[2,32]{1,0:T(2,128)}) custom-call(bf16[2,256,256]{2,1,0:T(8,128)(2,1)} %get-tuple-element.12.refs_0_, f32[2,256,256]{2,1,0:T(8,128)} %get-tuple-element.13.refs_1_, f32[2,6144]{1,0:T(2,128)} %get-tuple-element.14.refs_2_, ...), custom_call_target="tpu_custom_call" | custom-call | tf_op jit(solution)/shard_map/pallas_call | solution.py:947

commit v5 on v4

--- a/solution.py
+++ b/solution.py
@@ -94,7 +94,8 @@
         residue=vm((MICRO, WIDTH, NODES), F32),
         doubled=vm((BLOCKS, WIDTH, 128), F32),
         scores=vm((BLOCKS, STEPS, 8, LANES), F32),
-        share_grad=vm((MICRO, BLOCKS, STEPS, 8, LANES), F32),
+        low_shares=vm((BLOCKS, STEPS, 8, LANES), F32),
+        share_grad=vm((BLOCKS, STEPS, 8, LANES), F32),
         message=vm((MICRO, BLOCKS, WIDTH, 128), F32),
         normed=vm((4, WIDTH, NODES), F32),
         inverse=vm((4, 8, NODES), F32),
@@ -494,7 +495,9 @@
         raised = [jnp.exp(logits[i] - largest) * used[i] for i in range(STEPS)]
         scale = 1.0 / halves_sum(functools.reduce(jnp.add, raised))
         for i in range(STEPS):
-            s.shares[p, block, i] = raised[i] * scale
+            share = raised[i] * scale
+            s.shares[p, block, i] = share
+            s.low_shares[block, i] = share.astype(BF16).astype(F32)
 
     def pass_messages(p, m, block):
         for h in range(HEADS):
@@ -502,8 +505,7 @@
             total = jnp.zeros((HEAD_WIDTH, 128), F32)
             for step in range(STEPS):
                 for half in range(2):
-                    share = s.shares[p, block, step, h : h + 1, half * 128 : (half + 1) * 128]
-                    share = share.astype(BF16).astype(F32)
+                    share = s.low_shares[block, step, h : h + 1, half * 128 : (half + 1) * 128]
                     total = total + share * rows_of[block][p, 2 * step + half, rows].astype(F32)
             s.message[m, block, rows, :] = total
 
@@ -626,16 +628,17 @@
             grad = s.grad_out[m, block, rows, :]
             for half in range(2):
                 product = rows_of[block][p, 2 * step + half, rows].astype(F32) * grad
-                s.share_grad[m, block, step, h : h + 1, half * 128 : (half + 1) * 128] = (
+                s.share_grad[block, step, h : h + 1, half * 128 : (half + 1) * 128] = (
                     jnp.sum(product, axis=0, keepdims=True)
                 )
 
     def logit_grads(p, m, block):
         shares = [s.shares[p, block, i] for i in range(STEPS)]
-        grads = [s.share_grad[m, block, i] for i in range(STEPS)]
+        grads = [s.share_grad[block, i] for i in range(STEPS)]
         total = halves_sum(functools.reduce(jnp.add, [a * b for a, b in zip(shares, grads)]))
         for i in range(STEPS):
-            s.share_grad[m, block, i] = 0.8 * shares[i] * (grads[i] - total)
+            s.share_grad[block, i] = 0.8 * shares[i] * (grads[i] - total)
+            s.low_shares[block, i] = shares[i].astype(BF16).astype(F32)
 
     def make_terms(p, layer, m, block, pair):
         for h in range(HEADS):
@@ -650,12 +653,11 @@
                 z = rows_of[block][p, 4 * pair + part, rows].astype(F32) + wanted
                 t = jnp.tanh(z)
                 w = t + 1.5
-                logit_grad = s.share_grad[m, block, step, h : h + 1, half : half + 128]
+                logit_grad = s.share_grad[block, step, h : h + 1, half : half + 128]
                 attn_sum = attn_sum + logit_grad * (z * w)
                 slope = logit_grad * (w + z * (1.0 - t * t))
                 target_sum = target_sum + slope
-                share = s.shares[p, block, step, h : h + 1, half : half + 128]
-                share = share.astype(BF16).astype(F32)
+                share = s.low_shares[block, step, h : h + 1, half : half + 128]
                 terms[pair % 2][rows, part * 128 : (part + 1) * 128] = (
                     share * grad + attn * slope
                 ).astype(BF16)
@@ -687,10 +689,10 @@
         s.grad_ext[...] = jnp.zeros_like(s.grad_ext)
         all_share_grads(p, m, 1)
         for b in range(SMALLS):
-            if b == 1:
-                progress()
             if b + 1 < SMALLS:
                 all_share_grads(p, m, b + 2)
+            if b == 0:
+                progress()
             here = pl.ds(b * BIG, 256)
             for pair in range(STEPS // 2):
                 make_terms(p, layer, m, b + 1, pair)
@@ -785,6 +787,12 @@
             def _():
                 finalise(2, 1, 0)
 
+            if shared_weights:
+
+                @pl.when(jnp.logical_and(i == 1, m == 1))
+                def _():
+                    weights_on(1)
+
             through_norm(first + m, layer, m)
             big_back(first + m, layer, m)
 
@@ -801,11 +809,6 @@
 
             def progress():
                 reduce_on(first + m)
-                if shared_weights:
-
-                    @pl.when(jnp.logical_and(i == 1, m == 0))
-                    def _():
-                        weights_on(1)
 
             smalls_back(first + m, layer, m, progress)
             return inner
@@ -887,15 +890,26 @@
 
 
 def hand_over(*refs):
-    *arrays, sems = refs
-    count = len(arrays) // 2
-    copies = [
-        pltpu.make_async_copy(arrays[k], arrays[count + k], sems.at[k]) for k in range(count)
-    ]
-    for copy in copies:
-        copy.start()
-    for copy in copies:
-        copy.wait()
+    count = (len(refs) - 1) // 3
+    sources, places, rooms, sems = refs[:count], refs[count : 2 * count], refs[2 * count : -1], refs[-1]
+    moves = []
+    for source, place, room in zip(sources, places, rooms):
+        parts = [pl.ds(m, 1) for m in range(MICRO)] if len(source.shape) == 3 else [pl.ds(0, 2)]
+        for part in parts:
+            k = len(moves)
+            moves.append(
+                (
+                    pltpu.make_async_copy(source.at[part], room.at[part], sems.at[0, k]),
+                    pltpu.make_async_copy(room.at[part], place.at[part], sems.at[1, k]),
+                )
+            )
+    for inward, _ in moves:
+        inward.start()
+    for inward, outward in moves:
+        inward.wait()
+        outward.start()
+    for _, outward in moves:
+        outward.wait()
 
 
 def per_device(
@@ -948,8 +962,9 @@
             hand_over,
             out_shape=list(outputs.values()),
             in_specs=[in_hbm] * len(outputs),
-            out_specs=[in_vmem] * len(outputs),
-            scratch_shapes=[pltpu.SemaphoreType.DMA((len(outputs),))],
+            out_specs=[in_hbm] * len(outputs),
+            scratch_shapes=[pltpu.VMEM(x.shape, x.dtype) for x in outputs.values()]
+            + [pltpu.SemaphoreType.DMA((2, 2 * len(outputs)))],
         )(*results)
     layer_output, input_gradient, weight_sums, vector_sums = results
     if not shared_weights:

time: 103 us -> 102 us (level)
    pallas_call x1, Pallas kernels: 99.8 us -> 98.5 us  [per_device(): pl.pallas_call(functools.partial(step_kernel, depth, shared_weights, [*in...]
where the time goes in v5:
time: 102 us; the launch traced here: 101 us
  Pallas kernels  101 us (99%)
    pallas_call x1, Pallas kernels, per_device(): pl.pallas_call(functools.partial(step_kernel, depth, shared_weights, [*in...  98.5 us

profile of v5, /device:TPU:0, one launch (start us, length us, event | category | flops | bytes accessed | tf_op | source)
XLA Modules:
  0.0 101.4 jit_solution(7793054143646495395)
XLA Ops:
  0.6 98.5 %shard_map.93 = (bf16[2,256,256]{2,1,0:T(8,128)(2,1)}, f32[2,256,256]{2,1,0:T(8,128)}, f32[2,6144]{1,0:T(2,128)}, f32[2,32]{1,0:T(2,128)}) custom-call(bf16[2,256,256]{2,1,0:T(8,128)(2,1)} %bitcast.14, s32[2,32,256]{2,1,0:T(8,128)} %bitcast.16, s32[2,32,256]{2,1,0:T(8,128)} %bitcast.17, bf16[2,256,256]{2,1,0:T(8,128)(2,1)} %bitcast.15, ...), custom_call_target="tpu_custom_call" | custom-call | tf_op jit(solution)/shard_map/pallas_call | solution.py:948
  99.2 2.0 %shard_map.94 = (bf16[2,256,256]{2,1,0:T(8,128)(2,1)}, f32[2,256,256]{2,1,0:T(8,128)}, f32[2,6144]{1,0:T(2,128)}, f32[2,32]{1,0:T(2,128)}) custom-call(bf16[2,256,256]{2,1,0:T(8,128)(2,1)} %get-tuple-element.12.refs_0_, f32[2,256,256]{2,1,0:T(8,128)} %get-tuple-element.13.refs_1_, f32[2,6144]{1,0:T(2,128)} %get-tuple-element.14.refs_2_, ...), custom_call_target="tpu_custom_call" | custom-call | tf_op jit(solution)/shard_map/pallas_call | solution.py:961

commit v6 on v5

--- a/solution.py
+++ b/solution.py
@@ -796,11 +796,11 @@
             through_norm(first + m, layer, m)
             big_back(first + m, layer, m)
 
+            start(reduce_core(first + m))
+
             @pl.when(jnp.logical_and(i == 1, m == 1))
             def _():
                 s.head_weights[...] = tn(s.table[1], s.table[3])
-
-            start(reduce_core(first + m))
 
             @pl.when(jnp.logical_and(i == 1, m == 0))
             def _():
@@ -832,8 +832,7 @@
     pl.semaphore_wait(barrier, len(partners))
 
     if shared_weights:
-        for layer in range(LAYERS):
-            start(gather_pieces_z(layer))
+        start(gather_pieces_z(0))
     finish(bring(0, "features"))
     for m in range(MICRO):
         share(m, s.features[m])
@@ -854,13 +853,14 @@
     if shared_weights:
         finish(gather_pieces_z(0))
         start(gather_pieces_xy(0))
-        finish(gather_pieces_z(1))
+        start(gather_pieces_z(1))
         start(gather_far(0))
     if kept > 1:
         mark_big(0)
         mark_big(1)
     if shared_weights:
         finish(gather_pieces_xy(0))
+        finish(gather_pieces_z(1))
         start(gather_core(4))
         start(gather_pieces_xy(1))
         start(gather_far(1))

time: 102 us -> 101 us (level)
  no operation moved by 1% of the time
where the time goes in v6:
time: 101 us
  Pallas kernels  100 us (99%)
    pallas_call x1, Pallas kernels, per_device(): pl.pallas_call(functools.partial(step_kernel, depth, shared_weights, [*in...  98.2 us
    pallas_call x1, Pallas kernels, per_device(): pl.pallas_call(hand_over, out_shape=list(outputs.values()), in_specs=[in_...  2.02 us

profile of v6, /device:TPU:0, one launch (start us, length us, event | category | flops | bytes accessed | tf_op | source)
XLA Modules:
  0.0 101.0 jit_solution(4394806906099065550)
XLA Ops:
  0.6 98.2 %shard_map.93 = (bf16[2,256,256]{2,1,0:T(8,128)(2,1)}, f32[2,256,256]{2,1,0:T(8,128)}, f32[2,6144]{1,0:T(2,128)}, f32[2,32]{1,0:T(2,128)}) custom-call(bf16[2,256,256]{2,1,0:T(8,128)(2,1)} %bitcast.14, s32[2,32,256]{2,1,0:T(8,128)} %bitcast.16, s32[2,32,256]{2,1,0:T(8,128)} %bitcast.17, bf16[2,256,256]{2,1,0:T(8,128)(2,1)} %bitcast.15, ...), custom_call_target="tpu_custom_call" | custom-call | tf_op jit(solution)/shard_map/pallas_call | solution.py:948
  98.9 2.0 %shard_map.94 = (bf16[2,256,256]{2,1,0:T(8,128)(2,1)}, f32[2,256,256]{2,1,0:T(8,128)}, f32[2,6144]{1,0:T(2,128)}, f32[2,32]{1,0:T(2,128)}) custom-call(bf16[2,256,256]{2,1,0:T(8,128)(2,1)} %get-tuple-element.12.refs_0_, f32[2,256,256]{2,1,0:T(8,128)} %get-tuple-element.13.refs_1_, f32[2,6144]{1,0:T(2,128)} %get-tuple-element.14.refs_2_, ...), custom_call_target="tpu_custom_call" | custom-call | tf_op jit(solution)/shard_map/pallas_call | solution.py:961
